TPU v7x, 256 devices: a whole 4x4x8 slice. The times are simulated.
256 devices in a mesh: seq: 256 (over y, x, z, core).
Axes of the slice: x: 4, y: 4, z: 8, core: 2. Of those that a mesh axis runs over, the one named last changes fastest.
Arguments:
- queries: bfloat16 [256, 2, 256, 2048], P('seq'), may hold values from -12 to 12
- keys: bfloat16 [256, 2, 256, 512], P('seq'), may hold values from -4 to 4
- values: bfloat16 [256, 2, 256, 512], P('seq'), may hold values from -6 to 6
Outputs:
- attended: bfloat16 [256, 2, 256, 2048], P('seq')
All inputs are finite; a program needn't handle non-finite values.
Results may differ from a plain program's by a relative error of at most 0.0034.
Values may be sent and summed in bfloat16 or wider, within the bound.
No kernel may reach another device: no remote copies, remote signals or barrier semaphores. Data moves between devices by JAX's collectives and lax.ppermute only.
A program may use at most 64 MiB of HBM per device.

v0:
```python
import jax
import jax.numpy as jnp
from jax import lax
from jax.sharding import PartitionSpec as P

HEADS = 32
KV_HEADS = 8
HEAD_DIM = 64
BAND = 2


def shortened(shard):
    return jax.tree.map(lambda a: a.astype(jnp.bfloat16) if a.dtype == jnp.float32 else a, shard)


def from_behind(block, axis, distance):
    devices = range(lax.axis_size(axis))
    route = [(i - distance, i) for i in devices if i - distance in devices]
    return lax.ppermute(block, axis, route)


def attend(query, key_rows, value_rows, valid):
    length = query.shape[0]
    per_group = HEADS // KV_HEADS
    inverse_root = 1.0 / HEAD_DIM**0.5

    def one_group(group_index):
        query_group = lax.dynamic_slice_in_dim(
            query, group_index * per_group * HEAD_DIM, per_group * HEAD_DIM, 1
        )
        query_group = query_group.reshape(length, per_group, HEAD_DIM)
        key_group = lax.dynamic_slice_in_dim(key_rows, group_index * HEAD_DIM, HEAD_DIM, 1)
        value_group = lax.dynamic_slice_in_dim(value_rows, group_index * HEAD_DIM, HEAD_DIM, 1)
        scores = (
            jnp.einsum("qhd,kd->hqk", query_group, key_group, preferred_element_type=jnp.float32)
            * inverse_root
        )
        scores = jnp.where(valid[None], scores, jnp.float32(-1e30))
        peak = jnp.max(scores, axis=-1, keepdims=True)
        raw = jnp.exp(scores - peak)
        totals = jnp.sum(raw, axis=-1)
        weights = raw.astype(jnp.bfloat16)
        mixed = jnp.einsum("hqk,kd->qhd", weights, value_group, preferred_element_type=jnp.float32)
        mixed = mixed / totals.T[:, :, None]
        return mixed.reshape(length, per_group * HEAD_DIM)

    outputs = lax.map(one_group, jnp.arange(KV_HEADS, dtype=jnp.int32))
    return outputs.transpose(1, 0, 2).reshape(length, HEADS * HEAD_DIM).astype(jnp.bfloat16)


def band_mask(usable, length):
    causal = jnp.arange(length)[:, None] >= jnp.arange(length)[None, :]
    pieces = [jnp.broadcast_to(usable[offset], (length, length)) for offset in range(BAND, 0, -1)]
    return jnp.concatenate(pieces + [causal], axis=1)


def on_device(queries, keys, values):
    devices = lax.axis_size("seq")
    position = lax.axis_index("seq")
    is_last = position == devices - 1
    own_first = (keys[0, 0], values[0, 0])
    own_second = (keys[0, 1], values[0, 1])
    rising_list = [own_first]
    falling_list = [own_second]
    for offset in range(BAND):
        arrived_up = from_behind(shortened(rising_list[-1]), "seq", 1)
        arrived_down = from_behind(shortened(falling_list[-1]), "seq", -1)
        folded = tuple(
            (
                jnp.where(is_last, mine, theirs)
                for mine, theirs in zip(rising_list[-1], arrived_down)
            )
        )
        rising_list.append(arrived_up)
        falling_list.append(folded)
    length = queries.shape[2]
    first_keys = jnp.concatenate([rising_list[offset][0] for offset in range(BAND, -1, -1)], axis=0)
    first_values = jnp.concatenate(
        [rising_list[offset][1] for offset in range(BAND, -1, -1)], axis=0
    )
    second_keys = jnp.concatenate(
        [falling_list[offset][0] for offset in range(BAND, -1, -1)], axis=0
    )
    second_values = jnp.concatenate(
        [falling_list[offset][1] for offset in range(BAND, -1, -1)], axis=0
    )
    first_usable = [position >= offset for offset in range(BAND + 1)]
    second_usable = [jnp.bool_(True) for offset in range(BAND + 1)]
    first_out = attend(queries[0, 0], first_keys, first_values, band_mask(first_usable, length))
    second_out = attend(queries[0, 1], second_keys, second_values, band_mask(second_usable, length))
    return jnp.stack([first_out, second_out], axis=0)[None]


def solution(mesh):
    placed = (P("seq", None, None, None), P("seq", None, None, None), P("seq", None, None, None))
    return jax.shard_map(
        on_device, mesh=mesh, in_specs=placed, out_specs=P("seq", None, None, None), check_vma=False
    )
```

profile of v0, /device:TPU:24, one launch (start us, length us, event | category | flops | bytes accessed | tf_op | source)
XLA Modules:
  0.0 159.9 jit_solution(7483736151845743905)
XLA Ops:
  1.2 9.6 %collective-permute-start.6 = (bf16[256,512]{0,1:T(8,128)(2,1)S(1)}, bf16[256,512]{0,1:T(8,128)(2,1)}, u32[]{:S(2)}, u32[]{:S(2)}) collective-permute-start(bf16[256,512]{0,1:T(8,128)(2,1)S(1)} %bitcast.138), channel_id=1, source_target_pairs={{1,0},{2,1},{3,2},{4,3},{5,4},{6,5},{7,6},{8,7},{9,8},{10,9},{11,1... | collective-permute-start | bytes 786440 | tf_op jit(solution)/shard_map/ppermute | solution.py:19
  10.9 1.9 %collective-permute-start.2 = (bf16[256,512]{0,1:T(8,128)(2,1)S(1)}, bf16[256,512]{0,1:T(8,128)(2,1)}, u32[]{:S(2)}, u32[]{:S(2)}) collective-permute-start(bf16[256,512]{0,1:T(8,128)(2,1)S(1)} %bitcast.134), channel_id=1, source_target_pairs={{0,1},{1,2},{2,3},{3,4},{4,5},{5,6},{6,7},{7,8},{8,9},{9,10},{10,1... | collective-permute-start | bytes 786440 | tf_op jit(solution)/shard_map/ppermute | solution.py:19
  14.1 7.9 %collective-permute-start.4 = (bf16[256,512]{0,1:T(8,128)(2,1)S(1)}, bf16[256,512]{0,1:T(8,128)(2,1)}, u32[]{:S(2)}, u32[]{:S(2)}) collective-permute-start(bf16[256,512]{0,1:T(8,128)(2,1)S(1)} %bitcast.140), channel_id=1, source_target_pairs={{1,0},{2,1},{3,2},{4,3},{5,4},{6,5},{7,6},{8,7},{9,8},{10,9},{11,1... | collective-permute-start | bytes 786440 | tf_op jit(solution)/shard_map/ppermute | solution.py:19
  22.1 1.9 %collective-permute-start = (bf16[256,512]{0,1:T(8,128)(2,1)S(1)}, bf16[256,512]{0,1:T(8,128)(2,1)}, u32[]{:S(2)}, u32[]{:S(2)}) collective-permute-start(bf16[256,512]{0,1:T(8,128)(2,1)S(1)} %bitcast.136), channel_id=1, source_target_pairs={{0,1},{1,2},{2,3},{3,4},{4,5},{5,6},{6,7},{7,8},{8,9},{9,10},{10,1... | collective-permute-start | bytes 786440 | tf_op jit(solution)/shard_map/ppermute | solution.py:19
  27.6 7.8 %collective-permute-start.7 = (bf16[256,512]{0,1:T(8,128)(2,1)}, bf16[256,512]{0,1:T(8,128)(2,1)}, u32[]{:S(2)}, u32[]{:S(2)}) collective-permute-start(bf16[256,512]{0,1:T(8,128)(2,1)} %broadcast_select_fusion.1), channel_id=1, source_target_pairs={{1,0},{2,1},{3,2},{4,3},{5,4},{6,5},{7,6},{8,7},{9,8},{10,9},{11,1... | collective-permute-start | bytes 786440 | tf_op jit(solution)/shard_map/ppermute | solution.py:19
  38.5 1.9 %collective-permute-start.5 = (bf16[256,512]{0,1:T(8,128)(2,1)S(1)}, bf16[256,512]{0,1:T(8,128)(2,1)S(1)}, u32[]{:S(2)}, u32[]{:S(2)}) collective-permute-start(bf16[256,512]{0,1:T(8,128)(2,1)S(1)} %broadcast_select_fusion.3), channel_id=1, source_target_pairs={{1,0},{2,1},{3,2},{4,3},{5,4},{6,5},{7,6},{8,7},{9,8},{10,9},{11,1... | collective-permute-start | bytes 786440 | tf_op jit(solution)/shard_map/ppermute | solution.py:19
  40.4 2.4 %collective-permute-start.1 = (bf16[256,512]{0,1:T(8,128)(2,1)}, bf16[256,512]{0,1:T(8,128)(2,1)}, u32[]{:S(2)}, u32[]{:S(2)}) collective-permute-start(bf16[256,512]{0,1:T(8,128)(2,1)} %collective-permute-done), channel_id=1, source_target_pairs={{0,1},{1,2},{2,3},{3,4},{4,5},{5,6},{6,7},{7,8},{8,9},{9,10},{10,1... | collective-permute-start | bytes 786440 | tf_op jit(solution)/shard_map/ppermute | solution.py:19
  42.8 1.9 %collective-permute-start.3 = (bf16[256,512]{0,1:T(8,128)(2,1)}, bf16[256,512]{0,1:T(8,128)(2,1)}, u32[]{:S(2)}, u32[]{:S(2)}) collective-permute-start(bf16[256,512]{0,1:T(8,128)(2,1)} %collective-permute-done.2), channel_id=1, source_target_pairs={{0,1},{1,2},{2,3},{3,4},{4,5},{5,6},{6,7},{7,8},{8,9},{9,10},{10,1... | collective-permute-start | bytes 786440 | tf_op jit(solution)/shard_map/ppermute | solution.py:19
  45.8 1.9 %pad_maximum_fusion.3 = bf16[768,512]{0,1:T(8,128)(2,1)} fusion(bf16[256,512]{0,1:T(8,128)(2,1)S(1)} %bitcast.139, bf16[256,512]{0,1:T(8,128)(2,1)} %broadcast_select_fusion.1, bf16[256,512]{0,1:T(8,128)(2,1)S(1)} %broadcast_select_fusion), kind=kLoop, calls=%fused_computation.44 | loop fusion | flops 2359296 | bytes 1572864 | tf_op jit(solution)/shard_map/concatenate | solution.py:81
  48.7 55.2 %while.25 = (s32[]{:T(128)}, bf16[8,256,256]{1,2,0:T(8,128)(2,1)S(1)}, s32[8]{0:T(128)S(1)}, bf16[768,512]{0,1:T(8,128)(2,1)}, pred[256,768]{0,1:T(8,128)(4,1)S(...) while((s32[]{:T(128)}, ...), condition=%wide.region_7.8_spmd, body=%wide.region_4.7_spmd.sunk | while | flops 210106368 | bytes 11030773 | solution.py:47
  53.8 1.8 %fusion.70 = bf16[256,4,64]{0,2,1:T(8,128)(2,1)S(1)} fusion(f32[768,256,4]{1,0,2:T(8,128)S(1)} %get-tuple-element.317, f32[4,256]{1,0:T(4,128)S(1)} %get-tuple-element.318, pred[256,768]{0,1:T(8,128)(4,1)S(1)} %get-tuple-element.349, f32[256,4]{0,1:T(4,128)S(1)} %bitcast.142, bf16[768,512]{0,1:T(8,128)(2,1)} %get-tuple-element.348, s32[]{:T(128)S(6)} %select_n.115), kind=kOutput, calls=%fused_computation.28.clone.1 | convolution fusion | flops 103940096 | bytes 3579908 | tf_op jit(solution)/shard_map/while/body/eval_jaxpr/hqk,kd->qhd/dot_general | solution.py:43
  60.7 1.8 %fusion.70 = bf16[256,4,64]{0,2,1:T(8,128)(2,1)S(1)} fusion(f32[768,256,4]{1,0,2:T(8,128)S(1)} %get-tuple-element.317, f32[4,256]{1,0:T(4,128)S(1)} %get-tuple-element.318, pred[256,768]{0,1:T(8,128)(4,1)S(1)} %get-tuple-element.349, f32[256,4]{0,1:T(4,128)S(1)} %bitcast.142, bf16[768,512]{0,1:T(8,128)(2,1)} %get-tuple-element.348, s32[]{:T(128)S(6)} %select_n.115), kind=kOutput, calls=%fused_computation.28.clone.1 | convolution fusion | flops 103940096 | bytes 3579908 | tf_op jit(solution)/shard_map/while/body/eval_jaxpr/hqk,kd->qhd/dot_general | solution.py:43
  67.6 1.8 %fusion.70 = bf16[256,4,64]{0,2,1:T(8,128)(2,1)S(1)} fusion(f32[768,256,4]{1,0,2:T(8,128)S(1)} %get-tuple-element.317, f32[4,256]{1,0:T(4,128)S(1)} %get-tuple-element.318, pred[256,768]{0,1:T(8,128)(4,1)S(1)} %get-tuple-element.349, f32[256,4]{0,1:T(4,128)S(1)} %bitcast.142, bf16[768,512]{0,1:T(8,128)(2,1)} %get-tuple-element.348, s32[]{:T(128)S(6)} %select_n.115), kind=kOutput, calls=%fused_computation.28.clone.1 | convolution fusion | flops 103940096 | bytes 3579908 | tf_op jit(solution)/shard_map/while/body/eval_jaxpr/hqk,kd->qhd/dot_general | solution.py:43
  74.5 1.8 %fusion.70 = bf16[256,4,64]{0,2,1:T(8,128)(2,1)S(1)} fusion(f32[768,256,4]{1,0,2:T(8,128)S(1)} %get-tuple-element.317, f32[4,256]{1,0:T(4,128)S(1)} %get-tuple-element.318, pred[256,768]{0,1:T(8,128)(4,1)S(1)} %get-tuple-element.349, f32[256,4]{0,1:T(4,128)S(1)} %bitcast.142, bf16[768,512]{0,1:T(8,128)(2,1)} %get-tuple-element.348, s32[]{:T(128)S(6)} %select_n.115), kind=kOutput, calls=%fused_computation.28.clone.1 | convolution fusion | flops 103940096 | bytes 3579908 | tf_op jit(solution)/shard_map/while/body/eval_jaxpr/hqk,kd->qhd/dot_general | solution.py:43
  81.5 1.8 %fusion.70 = bf16[256,4,64]{0,2,1:T(8,128)(2,1)S(1)} fusion(f32[768,256,4]{1,0,2:T(8,128)S(1)} %get-tuple-element.317, f32[4,256]{1,0:T(4,128)S(1)} %get-tuple-element.318, pred[256,768]{0,1:T(8,128)(4,1)S(1)} %get-tuple-element.349, f32[256,4]{0,1:T(4,128)S(1)} %bitcast.142, bf16[768,512]{0,1:T(8,128)(2,1)} %get-tuple-element.348, s32[]{:T(128)S(6)} %select_n.115), kind=kOutput, calls=%fused_computation.28.clone.1 | convolution fusion | flops 103940096 | bytes 3579908 | tf_op jit(solution)/shard_map/while/body/eval_jaxpr/hqk,kd->qhd/dot_general | solution.py:43
  88.4 1.8 %fusion.70 = bf16[256,4,64]{0,2,1:T(8,128)(2,1)S(1)} fusion(f32[768,256,4]{1,0,2:T(8,128)S(1)} %get-tuple-element.317, f32[4,256]{1,0:T(4,128)S(1)} %get-tuple-element.318, pred[256,768]{0,1:T(8,128)(4,1)S(1)} %get-tuple-element.349, f32[256,4]{0,1:T(4,128)S(1)} %bitcast.142, bf16[768,512]{0,1:T(8,128)(2,1)} %get-tuple-element.348, s32[]{:T(128)S(6)} %select_n.115), kind=kOutput, calls=%fused_computation.28.clone.1 | convolution fusion | flops 103940096 | bytes 3579908 | tf_op jit(solution)/shard_map/while/body/eval_jaxpr/hqk,kd->qhd/dot_general | solution.py:43
  95.3 1.8 %fusion.70 = bf16[256,4,64]{0,2,1:T(8,128)(2,1)S(1)} fusion(f32[768,256,4]{1,0,2:T(8,128)S(1)} %get-tuple-element.317, f32[4,256]{1,0:T(4,128)S(1)} %get-tuple-element.318, pred[256,768]{0,1:T(8,128)(4,1)S(1)} %get-tuple-element.349, f32[256,4]{0,1:T(4,128)S(1)} %bitcast.142, bf16[768,512]{0,1:T(8,128)(2,1)} %get-tuple-element.348, s32[]{:T(128)S(6)} %select_n.115), kind=kOutput, calls=%fused_computation.28.clone.1 | convolution fusion | flops 103940096 | bytes 3579908 | tf_op jit(solution)/shard_map/while/body/eval_jaxpr/hqk,kd->qhd/dot_general | solution.py:43
  102.2 1.8 %fusion.70 = bf16[256,4,64]{0,2,1:T(8,128)(2,1)S(1)} fusion(f32[768,256,4]{1,0,2:T(8,128)S(1)} %get-tuple-element.317, f32[4,256]{1,0:T(4,128)S(1)} %get-tuple-element.318, pred[256,768]{0,1:T(8,128)(4,1)S(1)} %get-tuple-element.349, f32[256,4]{0,1:T(4,128)S(1)} %bitcast.142, bf16[768,512]{0,1:T(8,128)(2,1)} %get-tuple-element.348, s32[]{:T(128)S(6)} %select_n.115), kind=kOutput, calls=%fused_computation.28.clone.1 | convolution fusion | flops 103940096 | bytes 3579908 | tf_op jit(solution)/shard_map/while/body/eval_jaxpr/hqk,kd->qhd/dot_general | solution.py:43
  104.7 2.0 %pad_maximum_fusion = bf16[768,512]{0,1:T(8,128)(2,1)} fusion(bf16[256,512]{0,1:T(8,128)(2,1)} %bitcast.137, bf16[256,512]{0,1:T(8,128)(2,1)} %collective-permute-done, bf16[256,512]{0,1:T(8,128)(2,1)} %collective-permute-done.1), kind=kLoop, calls=%fused_computation.41 | loop fusion | flops 2359296 | bytes 1572864 | tf_op jit(solution)/shard_map/concatenate | solution.py:78
  106.7 2.1 %pad_maximum_fusion.1 = bf16[768,512]{0,1:T(8,128)(2,1)} fusion(bf16[256,512]{0,1:T(8,128)(2,1)} %bitcast.135, bf16[256,512]{0,1:T(8,128)(2,1)} %collective-permute-done.2, bf16[256,512]{0,1:T(8,128)(2,1)} %collective-permute-done.3), kind=kLoop, calls=%fused_computation.42 | loop fusion | flops 2359296 | bytes 1572864 | tf_op jit(solution)/shard_map/concatenate | solution.py:77
  108.8 48.9 %while.24 = (s32[]{:T(128)}, bf16[8,256,256]{1,2,0:T(8,128)(2,1)S(1)}, s32[8]{0:T(128)S(1)}, bf16[768,512]{0,1:T(8,128)(2,1)}, pred[256,768]{0,1:T(8,128)(4,1)S(...) while((s32[]{:T(128)}, ...), condition=%wide.region_3.4_spmd, body=%wide.region_0.3_spmd.sunk | while | flops 210106368 | bytes 11030773 | solution.py:47
  113.1 1.8 %fusion.64 = bf16[256,4,64]{0,2,1:T(8,128)(2,1)S(1)} fusion(f32[768,256,4]{1,0,2:T(8,128)S(1)} %get-tuple-element.308, f32[4,256]{1,0:T(4,128)S(1)} %get-tuple-element.309, pred[256,768]{0,1:T(8,128)(4,1)S(1)} %get-tuple-element.388, f32[256,4]{0,1:T(4,128)S(1)} %bitcast.143, bf16[768,512]{0,1:T(8,128)(2,1)} %get-tuple-element.387, s32[]{:T(128)S(6)} %select_n.110), kind=kOutput, calls=%fused_computation.8.clone.1 | convolution fusion | flops 103940096 | bytes 3579908 | tf_op jit(solution)/shard_map/while/body/eval_jaxpr/hqk,kd->qhd/dot_general | solution.py:43
  119.2 1.8 %fusion.64 = bf16[256,4,64]{0,2,1:T(8,128)(2,1)S(1)} fusion(f32[768,256,4]{1,0,2:T(8,128)S(1)} %get-tuple-element.308, f32[4,256]{1,0:T(4,128)S(1)} %get-tuple-element.309, pred[256,768]{0,1:T(8,128)(4,1)S(1)} %get-tuple-element.388, f32[256,4]{0,1:T(4,128)S(1)} %bitcast.143, bf16[768,512]{0,1:T(8,128)(2,1)} %get-tuple-element.387, s32[]{:T(128)S(6)} %select_n.110), kind=kOutput, calls=%fused_computation.8.clone.1 | convolution fusion | flops 103940096 | bytes 3579908 | tf_op jit(solution)/shard_map/while/body/eval_jaxpr/hqk,kd->qhd/dot_general | solution.py:43
  137.6 1.8 %fusion.64 = bf16[256,4,64]{0,2,1:T(8,128)(2,1)S(1)} fusion(f32[768,256,4]{1,0,2:T(8,128)S(1)} %get-tuple-element.308, f32[4,256]{1,0:T(4,128)S(1)} %get-tuple-element.309, pred[256,768]{0,1:T(8,128)(4,1)S(1)} %get-tuple-element.388, f32[256,4]{0,1:T(4,128)S(1)} %bitcast.143, bf16[768,512]{0,1:T(8,128)(2,1)} %get-tuple-element.387, s32[]{:T(128)S(6)} %select_n.110), kind=kOutput, calls=%fused_computation.8.clone.1 | convolution fusion | flops 103940096 | bytes 3579908 | tf_op jit(solution)/shard_map/while/body/eval_jaxpr/hqk,kd->qhd/dot_general | solution.py:43
  (123 shorter events, 76.8 us)
Async XLA Ops:
  1.2 24.6 %collective-permute-start.6 = (bf16[256,512]{0,1:T(8,128)(2,1)S(1)}, bf16[256,512]{0,1:T(8,128)(2,1)}, u32[]{:S(2)}, u32[]{:S(2)}) collective-permute-start(bf16[256,512]{0,1:T(8,128)(2,1)S(1)} %bitcast.138), channel_id=1, source_target_pairs={{1,0},{2,1},{3,2},{4,3},{5,4},{6,5},{7,6},{8,7},{9,8},{10,9},{11,1... | collective-permute-start | bytes 786440 | tf_op jit(solution)/shard_map/ppermute | solution.py:19
  10.9 14.9 %copy-start = (bf16[1,1,256,512]{2,3,1,0:T(8,128)(2,1)}, bf16[1,1,256,512]{2,3,1,0:T(8,128)(2,1)S(1)}, u32[]{:S(2)}) copy-start(bf16[1,1,256,512]{2,3,1,0:T(8,128)(2,1)S(1)} %copy.19) | copy-start | bytes 786436
  10.9 31.9 %collective-permute-start.2 = (bf16[256,512]{0,1:T(8,128)(2,1)S(1)}, bf16[256,512]{0,1:T(8,128)(2,1)}, u32[]{:S(2)}, u32[]{:S(2)}) collective-permute-start(bf16[256,512]{0,1:T(8,128)(2,1)S(1)} %bitcast.134), channel_id=1, source_target_pairs={{0,1},{1,2},{2,3},{3,4},{4,5},{5,6},{6,7},{7,8},{8,9},{9,10},{10,1... | collective-permute-start | bytes 786440 | tf_op jit(solution)/shard_map/ppermute | solution.py:19
  14.1 23.4 %collective-permute-start.4 = (bf16[256,512]{0,1:T(8,128)(2,1)S(1)}, bf16[256,512]{0,1:T(8,128)(2,1)}, u32[]{:S(2)}, u32[]{:S(2)}) collective-permute-start(bf16[256,512]{0,1:T(8,128)(2,1)S(1)} %bitcast.140), channel_id=1, source_target_pairs={{1,0},{2,1},{3,2},{4,3},{5,4},{6,5},{7,6},{8,7},{9,8},{10,9},{11,1... | collective-permute-start | bytes 786440 | tf_op jit(solution)/shard_map/ppermute | solution.py:19
  22.1 15.4 %copy-start.1 = (bf16[1,1,256,512]{2,3,1,0:T(8,128)(2,1)}, bf16[1,1,256,512]{2,3,1,0:T(8,128)(2,1)S(1)}, u32[]{:S(2)}) copy-start(bf16[1,1,256,512]{2,3,1,0:T(8,128)(2,1)S(1)} %copy.18) | copy-start | bytes 786436
  22.1 18.3 %collective-permute-start = (bf16[256,512]{0,1:T(8,128)(2,1)S(1)}, bf16[256,512]{0,1:T(8,128)(2,1)}, u32[]{:S(2)}, u32[]{:S(2)}) collective-permute-start(bf16[256,512]{0,1:T(8,128)(2,1)S(1)} %bitcast.136), channel_id=1, source_target_pairs={{0,1},{1,2},{2,3},{3,4},{4,5},{5,6},{6,7},{7,8},{8,9},{9,10},{10,1... | collective-permute-start | bytes 786440 | tf_op jit(solution)/shard_map/ppermute | solution.py:19
  27.6 17.2 %collective-permute-start.7 = (bf16[256,512]{0,1:T(8,128)(2,1)}, bf16[256,512]{0,1:T(8,128)(2,1)}, u32[]{:S(2)}, u32[]{:S(2)}) collective-permute-start(bf16[256,512]{0,1:T(8,128)(2,1)} %broadcast_select_fusion.1), channel_id=1, source_target_pairs={{1,0},{2,1},{3,2},{4,3},{5,4},{6,5},{7,6},{8,7},{9,8},{10,9},{11,1... | collective-permute-start | bytes 786440 | tf_op jit(solution)/shard_map/ppermute | solution.py:19
  38.5 9.2 %collective-permute-start.5 = (bf16[256,512]{0,1:T(8,128)(2,1)S(1)}, bf16[256,512]{0,1:T(8,128)(2,1)S(1)}, u32[]{:S(2)}, u32[]{:S(2)}) collective-permute-start(bf16[256,512]{0,1:T(8,128)(2,1)S(1)} %broadcast_select_fusion.3), channel_id=1, source_target_pairs={{1,0},{2,1},{3,2},{4,3},{5,4},{6,5},{7,6},{8,7},{9,8},{10,9},{11,1... | collective-permute-start | bytes 786440 | tf_op jit(solution)/shard_map/ppermute | solution.py:19
  40.4 64.2 %collective-permute-start.1 = (bf16[256,512]{0,1:T(8,128)(2,1)}, bf16[256,512]{0,1:T(8,128)(2,1)}, u32[]{:S(2)}, u32[]{:S(2)}) collective-permute-start(bf16[256,512]{0,1:T(8,128)(2,1)} %collective-permute-done), channel_id=1, source_target_pairs={{0,1},{1,2},{2,3},{3,4},{4,5},{5,6},{6,7},{7,8},{8,9},{9,10},{10,1... | collective-permute-start | bytes 786440 | tf_op jit(solution)/shard_map/ppermute | solution.py:19
  42.8 63.8 %collective-permute-start.3 = (bf16[256,512]{0,1:T(8,128)(2,1)}, bf16[256,512]{0,1:T(8,128)(2,1)}, u32[]{:S(2)}, u32[]{:S(2)}) collective-permute-start(bf16[256,512]{0,1:T(8,128)(2,1)} %collective-permute-done.2), channel_id=1, source_target_pairs={{0,1},{1,2},{2,3},{3,4},{4,5},{5,6},{6,7},{7,8},{8,9},{9,10},{10,1... | collective-permute-start | bytes 786440 | tf_op jit(solution)/shard_map/ppermute | solution.py:19
where the time goes:
time: 162 us; the launch traced here: 160 us
  matrix products  53.6 us (33%)
  starting transfers between devices  35.4 us (22%)
  local copies, waits for them, and re-layouts  25.5 us (16%)
  other arithmetic  23.4 us (14%)
  loops' own time  21.7 us (13%)
    ppermute x8, starting transfers between devices, from_behind(): return lax.ppermute(block, axis, route)  35.4 us
    dot_general x16, matrix products, one_group(): jnp.einsum('hqk,kd->qhd', weights, value_group, preferred_element_type=jn...  28.6 us
    dot_general x16, matrix products, one_group(): jnp.einsum('qhd,kd->hqk', query_group, key_group, preferred_element_type=...  25 us
    another operation x2, loops' own time, attend(): outputs = lax.map(one_group, jnp.arange(KV_HEADS, dtype=jnp.int32))  21.7 us
    reduce_sum x16, other arithmetic, one_group(): totals = jnp.sum(raw, axis=-1)  11 us
    dynamic_slice x16, local copies, waits for them, and re-layouts, attend(): outputs = lax.map(one_group, jnp.arange(KV_HEADS, dtype=jnp.int32))  10.1 us
    dynamic_slice x16, local copies, waits for them, and re-layouts, one_group(): lax.dynamic_slice_in_dim(query, group_index * per_group * HEAD_DIM, per_g...  7.48 us
    select_n x4, other arithmetic, on_device(): jnp.where(is_last, mine, theirs)  3.7 us
  transfers between devices with their start and end apart: 8, of which 0 were waited for; matrix products, arithmetic and copies ran while one was open for 37% of the time, Pallas kernels for 0%

commit v1 on v0

v1 whole, which is shorter than its diff:
```python
import functools

import jax
import jax.numpy as jnp
from jax import lax
from jax.experimental import pallas as pl
from jax.experimental.pallas import tpu as pltpu
from jax.sharding import PartitionSpec as P

HEADS = 32
KV_HEADS = 8
HEAD_DIM = 64
BLOCK = 256
WIDTH = HEADS * HEAD_DIM
KV_WIDTH = KV_HEADS * HEAD_DIM
LANES = 128
F32 = jnp.float32
BF16 = jnp.bfloat16
NT = (((1,), (1,)), ((), ()))
NN = (((1,), (0,)), ((), ()))
SCALE = 1.0 / HEAD_DIM**0.5
TOTAL_LOW = 2.0**-80
TOTAL_HIGH = 2.0**100
MIB = 2**20


def low_lanes(rows):
    return lax.broadcasted_iota(jnp.int32, (rows, LANES), 1) < HEAD_DIM


def key_value_tiles(kv_ref, group, valid):
    column = LANES * (group // 2)
    keys = kv_ref[:, column : column + LANES] * BF16(SCALE)
    values = kv_ref[:, KV_WIDTH + column : KV_WIDTH + column + LANES]
    low = low_lanes(BLOCK)
    keep = low if group % 2 == 0 else ~low
    keys = jnp.where(keep, keys, BF16(0))
    values = jnp.where(keep, values, BF16(1))
    if valid is not None:
        keys, values = keys * valid, values * valid
    keys_other, values_other = pltpu.roll(keys, HEAD_DIM, 1), pltpu.roll(values, HEAD_DIM, 1)
    if group % 2 == 0:
        return (keys, keys_other), (values, values_other)
    return (keys_other, keys), (values_other, values)


def group_queries(q_ref, slot, group):
    column = 2 * LANES * group
    return jnp.concatenate(
        [q_ref[0, slot, :, column : column + LANES], q_ref[0, slot, :, column + LANES : column + 2 * LANES]],
        axis=0,
    )


def partial_sums(queries, kv_ref, group, diagonal=False, valid=None):
    keys, values = key_value_tiles(kv_ref, group, valid)
    rows = queries.shape[0]
    sums = []
    for parity in range(2):
        scores = lax.dot_general(queries, keys[parity], NT, preferred_element_type=F32)
        if diagonal:
            row = lax.broadcasted_iota(jnp.int32, (rows, BLOCK), 0) % BLOCK
            scores = jnp.where(row >= lax.broadcasted_iota(jnp.int32, (rows, BLOCK), 1), scores, -1e30)
        raw = jnp.exp(scores).astype(BF16)
        sums.append(lax.dot_general(raw, values[parity], NN, preferred_element_type=F32))
    return sums


def normalized(sums):
    low = low_lanes(sums[0].shape[0])
    total = pltpu.roll(jnp.where(low, sums[1], sums[0]), HEAD_DIM, 1)
    out = (jnp.where(low, sums[0], sums[1]) / total).astype(BF16)
    off = jnp.where((total > TOTAL_LOW) & (total < TOTAL_HIGH), 0.0, 1.0)
    return out, jnp.max(off, axis=0, keepdims=True)


def own_blocks(q_ref, x_ref, y_ref, acc_x, acc_y):
    parity = lax.axis_index("seq") % 2
    for group in range(KV_HEADS):
        for slot, kv_ref, acc in ((parity, x_ref, acc_x), (1 - parity, y_ref, acc_y)):
            sums = partial_sums(group_queries(q_ref, slot, group), kv_ref, group, diagonal=True)
            acc[group, 0], acc[group, 1] = sums


def add_near_y(q_ref, s_ref, acc_in, acc_out):
    slot = 1 - lax.axis_index("seq") % 2
    for group in range(KV_HEADS):
        sums = partial_sums(group_queries(q_ref, slot, group), s_ref, group)
        for parity in range(2):
            acc_out[group, parity] = acc_in[group, parity] + sums[parity]


def valid_from(first):
    return jnp.where(lax.axis_index("seq") == first, 0.0, 1.0).astype(BF16)


def finish_y(q_ref, b_ref, acc_in, out_ref, off_ref):
    slot = 1 - lax.axis_index("seq") % 2
    off = jnp.zeros((1, LANES), F32)
    for group in range(KV_HEADS):
        sums = partial_sums(group_queries(q_ref, slot, group), b_ref, group, valid=valid_from(1))
        out, bad = normalized([acc_in[group, parity] + sums[parity] for parity in range(2)])
        off = jnp.maximum(off, bad)
        for half in range(2):
            column = LANES * (2 * group + half)
            out_ref[:, column : column + LANES] = out[BLOCK * half : BLOCK * (half + 1)]
    off_ref[...] = jnp.broadcast_to(off, (8, LANES))


def add_near_x(q_ref, c_ref, acc_in, acc_out):
    slot = lax.axis_index("seq") % 2
    for group in range(KV_HEADS):
        sums = partial_sums(group_queries(q_ref, slot, group), c_ref, group, valid=valid_from(0))
        for parity in range(2):
            acc_out[group, parity] = acc_in[group, parity] + sums[parity]


def exact_block(q_ref, slot, blocks, usable, out_ref):
    low = low_lanes(BLOCK)
    causal = lax.broadcasted_iota(jnp.int32, (BLOCK, BLOCK), 0) >= lax.broadcasted_iota(
        jnp.int32, (BLOCK, BLOCK), 1
    )

    def slab(index, carry):
        kv_column = pl.multiple_of(LANES * (index // 4), LANES)
        column = pl.multiple_of(LANES * index, LANES)
        in_low = (index // 2) % 2 == 0
        queries = q_ref[0, slot, :, pl.ds(column, LANES)].astype(F32)
        outs = []
        for head in range(2):
            mine = low if head == 0 else ~low
            query = jnp.where(mine, queries, 0.0)
            shift_by = jnp.where(in_low, 0, HEAD_DIM)
            at_low = query if head == 0 else pltpu.roll(query, HEAD_DIM, 1)
            at_high = pltpu.roll(at_low, HEAD_DIM, 1)
            query = jnp.where(shift_by == 0, at_low, at_high).astype(BF16)
            scores = []
            for block, ok in zip(blocks, usable):
                keys = block[:, pl.ds(kv_column, LANES)]
                part = lax.dot_general(query, keys, NT, preferred_element_type=F32) * SCALE
                scores.append(jnp.where(causal if ok is None else ok, part, -1e30))
            peak = functools.reduce(jnp.maximum, [jnp.max(part, axis=1, keepdims=True) for part in scores])
            total, mixed = 0.0, 0.0
            for block, part in zip(blocks, scores):
                raw = jnp.exp(part - peak)
                total = total + jnp.sum(raw, axis=1, keepdims=True)
                values = block[:, pl.ds(pl.multiple_of(KV_WIDTH + kv_column, LANES), LANES)]
                mixed = mixed + lax.dot_general(raw.astype(BF16), values, NN, preferred_element_type=F32)
            mixed = mixed / total
            at_low = jnp.where(in_low, mixed, pltpu.roll(mixed, HEAD_DIM, 1))
            outs.append(at_low if head == 0 else pltpu.roll(at_low, HEAD_DIM, 1))
        out_ref[:, pl.ds(column, LANES)] = jnp.where(low, outs[0], outs[1]).astype(BF16)
        return carry

    lax.fori_loop(0, WIDTH // LANES, slab, 0)


def finish_x(
    q_ref, x_ref, y_ref, s_ref, b_ref, c_ref, a_ref, acc_in, y_done, y_off, out_ref, x_out, y_out, x_sems, y_sem
):
    index = lax.axis_index("seq")
    slot = index % 2
    y_copy = pltpu.make_async_copy(y_done, out_ref.at[0, 1 - slot], y_sem)
    y_copy.start()
    off = jnp.max(y_off[...], axis=0, keepdims=True)
    copies = []
    for group in range(KV_HEADS):
        sums = partial_sums(group_queries(q_ref, slot, group), a_ref, group, valid=valid_from(0))
        out, bad = normalized([acc_in[group, parity] + sums[parity] for parity in range(2)])
        off = jnp.maximum(off, bad)
        for half in range(2):
            column = LANES * (2 * group + half)
            x_out[:, column : column + LANES] = out[BLOCK * half : BLOCK * (half + 1)]
        if group % 2 == 1:
            columns = pl.ds(4 * LANES * (group // 2), 4 * LANES)
            copies.append(
                pltpu.make_async_copy(
                    x_out.at[:, columns], out_ref.at[0, slot, :, columns], x_sems.at[group // 2]
                )
            )
            copies[-1].start()
    for copy in copies:
        copy.wait()
    y_copy.wait()

    @pl.when(jnp.max(off) > 0.0)
    def _():
        exact_block(q_ref, slot, (x_ref, c_ref, a_ref), (None, index != 0, index != 0), x_out)
        exact_block(q_ref, 1 - slot, (y_ref, s_ref, b_ref), (None, index >= 0, index != 1), y_out)
        again = (
            pltpu.make_async_copy(x_out, out_ref.at[0, slot], x_sems.at[0]),
            pltpu.make_async_copy(y_out, out_ref.at[0, 1 - slot], y_sem),
        )
        for copy in again:
            copy.start()
        for copy in again:
            copy.wait()


ACC = jax.ShapeDtypeStruct((KV_HEADS, 2, 2 * BLOCK, LANES), F32)
ROWS = jax.ShapeDtypeStruct((BLOCK, WIDTH), BF16)
OFF = jax.ShapeDtypeStruct((8, LANES), F32)


def call(kernel, inputs, outputs, units, **more):
    vmem = pl.BlockSpec(memory_space=pltpu.VMEM)
    more.setdefault("out_specs", [vmem] * len(outputs))
    return pl.pallas_call(
        kernel,
        in_specs=[vmem] * inputs,
        out_shape=outputs,
        compiler_params=pltpu.CompilerParams(vmem_limit_bytes=24 * MIB),
        cost_estimate=pl.CostEstimate(
            flops=units * 10**10,
            bytes_accessed=1024,
            transcendentals=1024,
        ),
        **more,
    )


def on_device(queries, keys, values):
    count = lax.axis_size("seq")
    parity = lax.axis_index("seq") % 2
    both = jnp.concatenate([keys[0], values[0]], axis=-1)
    x = lax.dynamic_index_in_dim(both, parity, 0, keepdims=False)
    y = lax.dynamic_index_in_dim(both, 1 - parity, 0, keepdims=False)
    evens, odds = list(range(0, count, 2)), list(range(1, count, 2))
    ring = evens + odds[::-1]
    forth = list(zip(ring, ring[1:] + ring[:1]))
    ring = odds + evens[::-1]
    back = list(zip(ring, ring[1:] + ring[:1]))
    swap = [(i, i ^ 1) for i in range(count)]
    b = lax.ppermute(y, "seq", back)
    s = lax.ppermute(x, "seq", swap)
    acc_x, acc_y = call(own_blocks, 3, [ACC, ACC], 2)(queries, x, y)
    x_late, acc_x = lax.optimization_barrier((x, acc_x))
    a = lax.ppermute(x_late, "seq", forth)
    (acc_y,) = call(add_near_y, 3, [ACC], 1)(queries, s, acc_y)
    b, acc_y = lax.optimization_barrier((b, acc_y))
    c = lax.ppermute(b, "seq", swap)
    y_done, y_off = call(finish_y, 3, [ROWS, OFF], 1)(queries, b, acc_y)
    (acc_x,) = call(add_near_x, 3, [ACC], 1)(queries, c, acc_x)
    return call(
        finish_x,
        10,
        jax.ShapeDtypeStruct(queries.shape, BF16),
        1,
        out_specs=pl.BlockSpec(memory_space=pl.ANY),
        scratch_shapes=[
            pltpu.VMEM((BLOCK, WIDTH), BF16),
            pltpu.VMEM((BLOCK, WIDTH), BF16),
            pltpu.SemaphoreType.DMA((KV_HEADS // 2,)),
            pltpu.SemaphoreType.DMA,
        ],
    )(queries, x, y, s, b, c, a, acc_x, y_done, y_off)


def solution(mesh):
    placed = P("seq", None, None, None)
    return jax.shard_map(on_device, mesh=mesh, in_specs=(placed,) * 3, out_specs=placed, check_vma=False)
```

time: 162 us -> 75.8 us (0.47); the launches traced: 160 us -> 75.7 us
  Pallas kernels: 0 us -> 58.3 us
  matrix products: 53.6 us -> 0 us
  starting transfers between devices: 35.4 us -> 8.87 us
  local copies, waits for them, and re-layouts: 25.5 us -> 1.59 us
  other arithmetic: 23.4 us -> 1.29 us
  loops' own time: 21.7 us -> 0 us
  waiting for transfers between devices: 0.02 us -> 5.46 us
    pallas_call x0 -> x5, Pallas kernels: none -> 58.3 us  [the longest x1 46.1 us: on_device(): call(finish_x, 10, jax.ShapeDtypeStruct(queries.shape, BF16), 1, out_spec...]
    dot_general x32 -> x0, matrix products: 53.6 us -> none  [the longest x16 28.6 us: one_group(): jnp.einsum('hqk,kd->qhd', weights, value_group, preferred_element_type=jn...]
    ppermute x8 -> x4, starting transfers between devices: 35.4 us -> 8.87 us  [the longest x1 8.31 us: on_device(): b = lax.ppermute(y, 'seq', back)]
    another operation x2 -> x0, loops' own time: 21.7 us -> none  [attend(): outputs = lax.map(one_group, jnp.arange(KV_HEADS, dtype=jnp.int32))]
    dynamic_slice x32 -> x0, local copies, waits for them, and re-layouts: 17.6 us -> none  [the longest x16 10.1 us: attend(): outputs = lax.map(one_group, jnp.arange(KV_HEADS, dtype=jnp.int32))]
    reduce_sum x16 -> x0, other arithmetic: 11 us -> none  [one_group(): totals = jnp.sum(raw, axis=-1)]
    concatenate x6 -> x0, other arithmetic: 7.15 us -> none  [the longest x1 2.05 us: on_device(): jnp.concatenate([rising_list[offset][0] for offset in range(BAND, -1, -1)...]
    ppermute x8 -> x4, waiting for transfers between devices: 0.02 us -> 5.46 us  [the longest x1 5.45 us: on_device(): a = lax.ppermute(x_late, 'seq', forth)]
  transfers between devices with their start and end apart: 8 -> 4, of which waited for: 0 -> 1; matrix products, arithmetic and copies ran while one was open for 37% -> 0% of each run, Pallas kernels for 0% -> 16%
where the time goes in v1:
time: 75.8 us; the launch traced here: 75.7 us
  Pallas kernels  58.3 us (77%)
  starting transfers between devices  8.87 us (12%)
  waiting for transfers between devices  5.46 us (7%)
  local copies, waits for them, and re-layouts  1.59 us (2%)
  other arithmetic  1.29 us (2%)
    pallas_call x1, Pallas kernels, on_device(): call(finish_x, 10, jax.ShapeDtypeStruct(queries.shape, BF16), 1, out_spec...  46.1 us
    ppermute x1, starting transfers between devices, on_device(): b = lax.ppermute(y, 'seq', back)  8.31 us
    ppermute x1, waiting for transfers between devices, on_device(): a = lax.ppermute(x_late, 'seq', forth)  5.45 us
    pallas_call x1, Pallas kernels, on_device(): acc_x, acc_y = call(own_blocks, 3, [ACC, ACC], 2)(queries, x, y)  4.64 us
    pallas_call x1, Pallas kernels, on_device(): y_done, y_off = call(finish_y, 3, [ROWS, OFF], 1)(queries, b, acc_y)  2.57 us
    pallas_call x1, Pallas kernels, on_device(): acc_x, = call(add_near_x, 3, [ACC], 1)(queries, c, acc_x)  2.47 us
    pallas_call x1, Pallas kernels, on_device(): acc_y, = call(add_near_y, 3, [ACC], 1)(queries, s, acc_y)  2.46 us
    unnamed x2, local copies, waits for them, and re-layouts  1.59 us
  transfers between devices with their start and end apart: 4, of which 1 were waited for; matrix products, arithmetic and copies ran while one was open for 0% of the time, Pallas kernels for 16%

profile of v1, /device:TPU:24, one launch (start us, length us, event | category | flops | bytes accessed | tf_op | source)
XLA Modules:
  0.0 75.7 jit_solution(4395835145426486012)
XLA Ops:
  0.0 1.3 %fusion.1 = (bf16[256,1024]{1,0:T(8,128)(2,1)S(1)}, bf16[256,1024]{1,0:T(8,128)(2,1)S(1)}) fusion(s32[]{:T(128)S(6)} %select_n.16, bf16[2,256,512]{2,1,0:T(8,128)(2,1)} %bitcast.6, bf16[2,256,512]{2,1,0:T(8,128)(2,1)} %bitcast.7, s32[]{:T(128)S(6)} %select_n.15), kind=kLoop, calls=%fused_computation.5 | loop fusion | flops 2097152 | bytes 2097160 | tf_op jit(solution)/shard_map/jit(dynamic_index_in_dim)/squeeze | solution.py:227
  1.3 0.1 collective-permute-start
  1.4 8.3 %collective-permute-start.1 = (bf16[256,1024]{1,0:T(8,128)(2,1)S(1)}, bf16[256,1024]{1,0:T(8,128)(2,1)S(1)}, u32[]{:S(2)}, u32[]{:S(2)}) collective-permute-start(bf16[256,1024]{1,0:T(8,128)(2,1)S(1)} %get-tuple-element.21.y_ref), channel_id=1, source_target_pairs={{1,3},{3,5},{5,7},{7,9},{9,11},{11,13},{13,15},{15,17},{17,19},{19... | collective-permute-start | bytes 1572872 | tf_op jit(solution)/shard_map/ppermute | solution.py:234
  9.7 0.0 copy-start
  9.7 1.6 %copy-done = bf16[1,2,256,2048]{3,2,1,0:T(8,128)(2,1)S(1)} copy-done((bf16[1,2,256,2048]{3,2,1,0:T(8,128)(2,1)S(1)}, bf16[1,2,256,2048]{3,2,1,0:T(8,128)(2,1)}, u32[]{:S(2)}) %copy-start) | copy-done | bytes 2097176
  11.3 4.6 %shard_map.37 = (f32[8,2,512,128]{3,2,1,0:T(8,128)S(1)}, f32[8,2,512,128]{3,2,1,0:T(8,128)S(1)}) custom-call(bf16[1,2,256,2048]{3,2,1,0:T(8,128)(2,1)S(1)} %copy-done, bf16[256,1024]{1,0:T(8,128)(2,1)S(1)} %get-tuple-element.16.x_ref, bf16[256,1024]{1,0:T(8,128)(2,1)S(1)} %get-tuple-element.21.y_ref), custom_call_target="tpu_custom_call" | custom-call | flops 20000000000 | bytes 1024 | tf_op jit(solution)/shard_map/pallas_call | solution.py:236
  15.9 0.1 collective-permute-start.3
  16.0 0.0 collective-permute-done.s_ref
  16.0 2.5 %shard_map.38.acc_in = f32[8,2,512,128]{3,2,1,0:T(8,128)S(1)} custom-call(bf16[1,2,256,2048]{3,2,1,0:T(8,128)(2,1)S(1)} %copy-done, bf16[256,1024]{1,0:T(8,128)(2,1)S(1)} %collective-permute-done.s_ref, f32[8,2,512,128]{3,2,1,0:T(8,128)S(1)} %get-tuple-element.13.acc_in), custom_call_target="tpu_custom_call" | custom-call | flops 10000000000 | bytes 1024 | tf_op jit(solution)/shard_map/pallas_call | solution.py:239
  18.5 0.0 collective-permute-done.1.b_ref
  18.5 0.4 collective-permute-start.2
  18.9 2.6 %shard_map.40 = (bf16[256,2048]{1,0:T(8,128)(2,1)S(1)}, f32[8,128]{1,0:T(8,128)S(1)}) custom-call(bf16[1,2,256,2048]{3,2,1,0:T(8,128)(2,1)S(1)} %copy-done, bf16[256,1024]{1,0:T(8,128)(2,1)S(1)} %collective-permute-done.1.b_ref, f32[8,2,512,128]{3,2,1,0:T(8,128)S(1)} %shard_map.38.acc_in), custom_call_target="tpu_custom_call" | custom-call | flops 10000000000 | bytes 1024 | tf_op jit(solution)/shard_map/pallas_call | solution.py:242
  21.5 0.0 collective-permute-done.2.c_ref
  21.5 2.5 %shard_map.39.acc_in = f32[8,2,512,128]{3,2,1,0:T(8,128)S(1)} custom-call(bf16[1,2,256,2048]{3,2,1,0:T(8,128)(2,1)S(1)} %copy-done, bf16[256,1024]{1,0:T(8,128)(2,1)S(1)} %collective-permute-done.2.c_ref, f32[8,2,512,128]{3,2,1,0:T(8,128)S(1)} %get-tuple-element.17.acc_in), custom_call_target="tpu_custom_call" | custom-call | flops 10000000000 | bytes 1024 | tf_op jit(solution)/shard_map/pallas_call | solution.py:243
  24.0 5.5 %collective-permute-done.3.a_ref = bf16[256,1024]{1,0:T(8,128)(2,1)S(1)} collective-permute-done((bf16[256,1024]{1,0:T(8,128)(2,1)S(1)}, bf16[256,1024]{1,0:T(8,128)(2,1)S(1)}, u32[]{:S(2)}, u32[]{:S(2)}) %collective-permute-start.3) | collective-permute-done | bytes 524320 | tf_op jit(solution)/shard_map/ppermute | solution.py:238
  29.4 46.1 %shard_map.41 = bf16[1,2,256,2048]{3,2,1,0:T(8,128)(2,1)} custom-call(bf16[1,2,256,2048]{3,2,1,0:T(8,128)(2,1)S(1)} %copy-done, bf16[256,1024]{1,0:T(8,128)(2,1)S(1)} %get-tuple-element.16.x_ref, bf16[256,1024]{1,0:T(8,128)(2,1)S(1)} %get-tuple-element.21.y_ref, bf16[256,1024]{1,0:T(8,128)(2,1)S(1)} %collective-permute-done.s_ref, ...), custom_call_target="tpu_custom_call" | custom-call | flops 10000000000 | bytes 1024 | tf_op jit(solution)/shard_map/pallas_call | solution.py:244
Async XLA Ops:
  1.3 14.7 %collective-permute-start = (bf16[256,1024]{1,0:T(8,128)(2,1)S(1)}, bf16[256,1024]{1,0:T(8,128)(2,1)S(1)}, u32[]{:S(2)}, u32[]{:S(2)}) collective-permute-start(bf16[256,1024]{1,0:T(8,128)(2,1)S(1)} %get-tuple-element.16.x_ref), channel_id=1, source_target_pairs={{0,1},{1,0},{2,3},{3,2},{4,5},{5,4},{6,7},{7,6},{8,9},{9,8},{10,11... | collective-permute-start | bytes 1572872 | tf_op jit(solution)/shard_map/ppermute | solution.py:235
  1.4 17.1 %collective-permute-start.1 = (bf16[256,1024]{1,0:T(8,128)(2,1)S(1)}, bf16[256,1024]{1,0:T(8,128)(2,1)S(1)}, u32[]{:S(2)}, u32[]{:S(2)}) collective-permute-start(bf16[256,1024]{1,0:T(8,128)(2,1)S(1)} %get-tuple-element.21.y_ref), channel_id=1, source_target_pairs={{1,3},{3,5},{5,7},{7,9},{9,11},{11,13},{13,15},{15,17},{17,19},{19... | collective-permute-start | bytes 1572872 | tf_op jit(solution)/shard_map/ppermute | solution.py:234
  9.7 1.6 %copy-start = (bf16[1,2,256,2048]{3,2,1,0:T(8,128)(2,1)S(1)}, bf16[1,2,256,2048]{3,2,1,0:T(8,128)(2,1)}, u32[]{:S(2)}) copy-start(bf16[1,2,256,2048]{3,2,1,0:T(8,128)(2,1)} %q_ref.9) | copy-start | bytes 6291460
  15.9 13.5 %collective-permute-start.3 = (bf16[256,1024]{1,0:T(8,128)(2,1)S(1)}, bf16[256,1024]{1,0:T(8,128)(2,1)S(1)}, u32[]{:S(2)}, u32[]{:S(2)}) collective-permute-start(bf16[256,1024]{1,0:T(8,128)(2,1)S(1)} %get-tuple-element.16.x_ref), channel_id=1, source_target_pairs={{0,2},{2,4},{4,6},{6,8},{8,10},{10,12},{12,14},{14,16},{16,18},{18... | collective-permute-start | bytes 1572872 | tf_op jit(solution)/shard_map/ppermute | solution.py:238
  18.5 3.0 %collective-permute-start.2 = (bf16[256,1024]{1,0:T(8,128)(2,1)S(1)}, bf16[256,1024]{1,0:T(8,128)(2,1)S(1)}, u32[]{:S(2)}, u32[]{:S(2)}) collective-permute-start(bf16[256,1024]{1,0:T(8,128)(2,1)S(1)} %collective-permute-done.1.b_ref), channel_id=1, source_target_pairs={{0,1},{1,0},{2,3},{3,2},{4,5},{5,4},{6,7},{7,6},{8,9},{9,8},{10,11... | collective-permute-start | bytes 1572872 | tf_op jit(solution)/shard_map/ppermute | solution.py:241

commit v2 on v1

--- a/solution.py
+++ b/solution.py
@@ -22,6 +22,7 @@
 TOTAL_LOW = 2.0**-80
 TOTAL_HIGH = 2.0**100
 MIB = 2**20
+FLOPS = 10**10
 
 
 def low_lanes(rows):
@@ -52,17 +53,22 @@
     )
 
 
-def partial_sums(queries, kv_ref, group, diagonal=False, valid=None):
-    keys, values = key_value_tiles(kv_ref, group, valid)
+def partial_sums(queries, kv_refs, group, diagonal=False, valid=None):
+    tiles = [key_value_tiles(kv_ref, group, valid) for kv_ref in kv_refs]
     rows = queries.shape[0]
     sums = []
     for parity in range(2):
-        scores = lax.dot_general(queries, keys[parity], NT, preferred_element_type=F32)
+        keys, values = (
+            jnp.concatenate([tile[kind][parity] for tile in tiles], axis=0) for kind in range(2)
+        )
+        scores = lax.dot_general(queries, keys, NT, preferred_element_type=F32)
         if diagonal:
             row = lax.broadcasted_iota(jnp.int32, (rows, BLOCK), 0) % BLOCK
-            scores = jnp.where(row >= lax.broadcasted_iota(jnp.int32, (rows, BLOCK), 1), scores, -1e30)
+            causal = row >= lax.broadcasted_iota(jnp.int32, (rows, BLOCK), 1)
+            own = jnp.where(causal, scores[:, :BLOCK], -1e30)
+            scores = jnp.concatenate([own, scores[:, BLOCK:]], axis=1) if len(kv_refs) > 1 else own
         raw = jnp.exp(scores).astype(BF16)
-        sums.append(lax.dot_general(raw, values[parity], NN, preferred_element_type=F32))
+        sums.append(lax.dot_general(raw, values, NN, preferred_element_type=F32))
     return sums
 
 
@@ -74,20 +80,18 @@
     return out, jnp.max(off, axis=0, keepdims=True)
 
 
-def own_blocks(q_ref, x_ref, y_ref, acc_x, acc_y):
-    parity = lax.axis_index("seq") % 2
-    for group in range(KV_HEADS):
-        for slot, kv_ref, acc in ((parity, x_ref, acc_x), (1 - parity, y_ref, acc_y)):
-            sums = partial_sums(group_queries(q_ref, slot, group), kv_ref, group, diagonal=True)
-            acc[group, 0], acc[group, 1] = sums
-
-
-def add_near_y(q_ref, s_ref, acc_in, acc_out):
+def start_x(q_ref, x_ref, acc):
+    slot = lax.axis_index("seq") % 2
+    for group in range(KV_HEADS):
+        sums = partial_sums(group_queries(q_ref, slot, group), [x_ref], group, diagonal=True)
+        acc[group, 0], acc[group, 1] = sums
+
+
+def start_y(q_ref, y_ref, s_ref, acc):
     slot = 1 - lax.axis_index("seq") % 2
     for group in range(KV_HEADS):
-        sums = partial_sums(group_queries(q_ref, slot, group), s_ref, group)
-        for parity in range(2):
-            acc_out[group, parity] = acc_in[group, parity] + sums[parity]
+        sums = partial_sums(group_queries(q_ref, slot, group), [y_ref, s_ref], group, diagonal=True)
+        acc[group, 0], acc[group, 1] = sums
 
 
 def valid_from(first):
@@ -98,7 +102,7 @@
     slot = 1 - lax.axis_index("seq") % 2
     off = jnp.zeros((1, LANES), F32)
     for group in range(KV_HEADS):
-        sums = partial_sums(group_queries(q_ref, slot, group), b_ref, group, valid=valid_from(1))
+        sums = partial_sums(group_queries(q_ref, slot, group), [b_ref], group, valid=valid_from(1))
         out, bad = normalized([acc_in[group, parity] + sums[parity] for parity in range(2)])
         off = jnp.maximum(off, bad)
         for half in range(2):
@@ -110,7 +114,7 @@
 def add_near_x(q_ref, c_ref, acc_in, acc_out):
     slot = lax.axis_index("seq") % 2
     for group in range(KV_HEADS):
-        sums = partial_sums(group_queries(q_ref, slot, group), c_ref, group, valid=valid_from(0))
+        sums = partial_sums(group_queries(q_ref, slot, group), [c_ref], group, valid=valid_from(0))
         for parity in range(2):
             acc_out[group, parity] = acc_in[group, parity] + sums[parity]
 
@@ -165,7 +169,7 @@
     off = jnp.max(y_off[...], axis=0, keepdims=True)
     copies = []
     for group in range(KV_HEADS):
-        sums = partial_sums(group_queries(q_ref, slot, group), a_ref, group, valid=valid_from(0))
+        sums = partial_sums(group_queries(q_ref, slot, group), [a_ref], group, valid=valid_from(0))
         out, bad = normalized([acc_in[group, parity] + sums[parity] for parity in range(2)])
         off = jnp.maximum(off, bad)
         for half in range(2):
@@ -211,7 +215,7 @@
         out_shape=outputs,
         compiler_params=pltpu.CompilerParams(vmem_limit_bytes=24 * MIB),
         cost_estimate=pl.CostEstimate(
-            flops=units * 10**10,
+            flops=units * FLOPS,
             bytes_accessed=1024,
             transcendentals=1024,
         ),
@@ -233,10 +237,10 @@
     swap = [(i, i ^ 1) for i in range(count)]
     b = lax.ppermute(y, "seq", back)
     s = lax.ppermute(x, "seq", swap)
-    acc_x, acc_y = call(own_blocks, 3, [ACC, ACC], 2)(queries, x, y)
+    (acc_x,) = call(start_x, 2, [ACC], 1)(queries, x)
     x_late, acc_x = lax.optimization_barrier((x, acc_x))
     a = lax.ppermute(x_late, "seq", forth)
-    (acc_y,) = call(add_near_y, 3, [ACC], 1)(queries, s, acc_y)
+    (acc_y,) = call(start_y, 3, [ACC], 2)(queries, y, s)
     b, acc_y = lax.optimization_barrier((b, acc_y))
     c = lax.ppermute(b, "seq", swap)
     y_done, y_off = call(finish_y, 3, [ROWS, OFF], 1)(queries, b, acc_y)

time: 75.8 us -> 73.5 us (0.970)
  waiting for transfers between devices: 5.46 us -> 2.19 us
  starting transfers between devices: 8.87 us -> 9.88 us
    ppermute x1, waiting for transfers between devices: 5.45 us -> 2.18 us  [on_device(): a = lax.ppermute(x_late, 'seq', forth)]
    ppermute x1, starting transfers between devices: 0.39 us -> 1.48 us  [on_device(): c = lax.ppermute(b, 'seq', swap)]
  transfers between devices with their start and end apart: 4 -> 4, of which waited for: 1 -> 1; matrix products, arithmetic and copies ran while one was open for 0% -> 0% of each run, Pallas kernels for 16% -> 17%
where the time goes in v2:
time: 73.5 us; the launch traced here: 73.4 us
  Pallas kernels  58.2 us (79%)
  starting transfers between devices  9.88 us (13%)
  waiting for transfers between devices  2.19 us (3%)
  local copies, waits for them, and re-layouts  1.59 us (2%)
  other arithmetic  1.29 us (2%)
    pallas_call x1, Pallas kernels, on_device(): call(finish_x, 10, jax.ShapeDtypeStruct(queries.shape, BF16), 1, out_spec...  46.1 us
    ppermute x1, starting transfers between devices, on_device(): b = lax.ppermute(y, 'seq', back)  8.31 us
    pallas_call x1, Pallas kernels, on_device(): acc_y, = call(start_y, 3, [ACC], 2)(queries, y, s)  4.64 us
    pallas_call x1, Pallas kernels, on_device(): y_done, y_off = call(finish_y, 3, [ROWS, OFF], 1)(queries, b, acc_y)  2.57 us
    pallas_call x1, Pallas kernels, on_device(): acc_x, = call(add_near_x, 3, [ACC], 1)(queries, c, acc_x)  2.47 us
    pallas_call x1, Pallas kernels, on_device(): acc_x, = call(start_x, 2, [ACC], 1)(queries, x)  2.45 us
    ppermute x1, waiting for transfers between devices, on_device(): a = lax.ppermute(x_late, 'seq', forth)  2.18 us
    unnamed x2, local copies, waits for them, and re-layouts  1.59 us
  transfers between devices with their start and end apart: 4, of which 1 were waited for; matrix products, arithmetic and copies ran while one was open for 0% of the time, Pallas kernels for 17%

profile of v2, /device:TPU:24, one launch (start us, length us, event | category | flops | bytes accessed | tf_op | source)
XLA Modules:
  0.0 73.4 jit_solution(16649890807217353097)
XLA Ops:
  0.0 1.3 %fusion.1 = (bf16[256,1024]{1,0:T(8,128)(2,1)S(1)}, bf16[256,1024]{1,0:T(8,128)(2,1)S(1)}) fusion(s32[]{:T(128)S(6)} %select_n.16, bf16[2,256,512]{2,1,0:T(8,128)(2,1)} %bitcast.6, bf16[2,256,512]{2,1,0:T(8,128)(2,1)} %bitcast.7, s32[]{:T(128)S(6)} %select_n.15), kind=kLoop, calls=%fused_computation.5 | loop fusion | flops 2097152 | bytes 2097160 | tf_op jit(solution)/shard_map/jit(dynamic_index_in_dim)/squeeze | solution.py:231
  1.3 8.3 %collective-permute-start.1 = (bf16[256,1024]{1,0:T(8,128)(2,1)S(1)}, bf16[256,1024]{1,0:T(8,128)(2,1)S(1)}, u32[]{:S(2)}, u32[]{:S(2)}) collective-permute-start(bf16[256,1024]{1,0:T(8,128)(2,1)S(1)} %get-tuple-element.17.y_ref), channel_id=1, source_target_pairs={{1,3},{3,5},{5,7},{7,9},{9,11},{11,13},{13,15},{15,17},{17,19},{19... | collective-permute-start | bytes 1572872 | tf_op jit(solution)/shard_map/ppermute | solution.py:238
  9.6 0.0 collective-permute-start
  9.6 0.0 copy-start
  9.6 1.6 %copy-done = bf16[1,2,256,2048]{3,2,1,0:T(8,128)(2,1)S(1)} copy-done((bf16[1,2,256,2048]{3,2,1,0:T(8,128)(2,1)S(1)}, bf16[1,2,256,2048]{3,2,1,0:T(8,128)(2,1)}, u32[]{:S(2)}) %copy-start) | copy-done | bytes 2097176
  11.2 2.5 %shard_map.38.acc_in = f32[8,2,512,128]{3,2,1,0:T(8,128)S(1)} custom-call(bf16[1,2,256,2048]{3,2,1,0:T(8,128)(2,1)S(1)} %copy-done, bf16[256,1024]{1,0:T(8,128)(2,1)S(1)} %get-tuple-element.12.x_ref), custom_call_target="tpu_custom_call" | custom-call | flops 10000000000 | bytes 1024 | tf_op jit(solution)/shard_map/pallas_call | solution.py:240
  13.7 0.1 collective-permute-start.3
  13.8 0.0 collective-permute-done.s_ref
  13.8 4.6 %shard_map.37.acc_in = f32[8,2,512,128]{3,2,1,0:T(8,128)S(1)} custom-call(bf16[1,2,256,2048]{3,2,1,0:T(8,128)(2,1)S(1)} %copy-done, bf16[256,1024]{1,0:T(8,128)(2,1)S(1)} %get-tuple-element.17.y_ref, bf16[256,1024]{1,0:T(8,128)(2,1)S(1)} %collective-permute-done.s_ref), custom_call_target="tpu_custom_call" | custom-call | flops 20000000000 | bytes 1024 | tf_op jit(solution)/shard_map/pallas_call | solution.py:243
  18.4 0.0 collective-permute-done.1.b_ref
  18.4 1.5 %collective-permute-start.2 = (bf16[256,1024]{1,0:T(8,128)(2,1)S(1)}, bf16[256,1024]{1,0:T(8,128)(2,1)S(1)}, u32[]{:S(2)}, u32[]{:S(2)}) collective-permute-start(bf16[256,1024]{1,0:T(8,128)(2,1)S(1)} %collective-permute-done.1.b_ref), channel_id=1, source_target_pairs={{0,1},{1,0},{2,3},{3,2},{4,5},{5,4},{6,7},{7,6},{8,9},{9,8},{10,11... | collective-permute-start | bytes 1572872 | tf_op jit(solution)/shard_map/ppermute | solution.py:245
  19.9 2.6 %shard_map.40 = (bf16[256,2048]{1,0:T(8,128)(2,1)S(1)}, f32[8,128]{1,0:T(8,128)S(1)}) custom-call(bf16[1,2,256,2048]{3,2,1,0:T(8,128)(2,1)S(1)} %copy-done, bf16[256,1024]{1,0:T(8,128)(2,1)S(1)} %collective-permute-done.1.b_ref, f32[8,2,512,128]{3,2,1,0:T(8,128)S(1)} %shard_map.37.acc_in), custom_call_target="tpu_custom_call" | custom-call | flops 10000000000 | bytes 1024 | tf_op jit(solution)/shard_map/pallas_call | solution.py:246
  22.5 0.0 collective-permute-done.2.c_ref
  22.5 2.5 %shard_map.39.acc_in = f32[8,2,512,128]{3,2,1,0:T(8,128)S(1)} custom-call(bf16[1,2,256,2048]{3,2,1,0:T(8,128)(2,1)S(1)} %copy-done, bf16[256,1024]{1,0:T(8,128)(2,1)S(1)} %collective-permute-done.2.c_ref, f32[8,2,512,128]{3,2,1,0:T(8,128)S(1)} %shard_map.38.acc_in), custom_call_target="tpu_custom_call" | custom-call | flops 10000000000 | bytes 1024 | tf_op jit(solution)/shard_map/pallas_call | solution.py:247
  25.0 2.2 %collective-permute-done.3.a_ref = bf16[256,1024]{1,0:T(8,128)(2,1)S(1)} collective-permute-done((bf16[256,1024]{1,0:T(8,128)(2,1)S(1)}, bf16[256,1024]{1,0:T(8,128)(2,1)S(1)}, u32[]{:S(2)}, u32[]{:S(2)}) %collective-permute-start.3) | collective-permute-done | bytes 524320 | tf_op jit(solution)/shard_map/ppermute | solution.py:242
  27.1 46.1 %shard_map.41 = bf16[1,2,256,2048]{3,2,1,0:T(8,128)(2,1)} custom-call(bf16[1,2,256,2048]{3,2,1,0:T(8,128)(2,1)S(1)} %copy-done, bf16[256,1024]{1,0:T(8,128)(2,1)S(1)} %get-tuple-element.12.x_ref, bf16[256,1024]{1,0:T(8,128)(2,1)S(1)} %get-tuple-element.17.y_ref, bf16[256,1024]{1,0:T(8,128)(2,1)S(1)} %collective-permute-done.s_ref, ...), custom_call_target="tpu_custom_call" | custom-call | flops 10000000000 | bytes 1024 | tf_op jit(solution)/shard_map/pallas_call | solution.py:248
Async XLA Ops:
  1.3 17.1 %collective-permute-start.1 = (bf16[256,1024]{1,0:T(8,128)(2,1)S(1)}, bf16[256,1024]{1,0:T(8,128)(2,1)S(1)}, u32[]{:S(2)}, u32[]{:S(2)}) collective-permute-start(bf16[256,1024]{1,0:T(8,128)(2,1)S(1)} %get-tuple-element.17.y_ref), channel_id=1, source_target_pairs={{1,3},{3,5},{5,7},{7,9},{9,11},{11,13},{13,15},{15,17},{17,19},{19... | collective-permute-start | bytes 1572872 | tf_op jit(solution)/shard_map/ppermute | solution.py:238
  9.6 4.1 %collective-permute-start = (bf16[256,1024]{1,0:T(8,128)(2,1)S(1)}, bf16[256,1024]{1,0:T(8,128)(2,1)S(1)}, u32[]{:S(2)}, u32[]{:S(2)}) collective-permute-start(bf16[256,1024]{1,0:T(8,128)(2,1)S(1)} %get-tuple-element.12.x_ref), channel_id=1, source_target_pairs={{0,1},{1,0},{2,3},{3,2},{4,5},{5,4},{6,7},{7,6},{8,9},{9,8},{10,11... | collective-permute-start | bytes 1572872 | tf_op jit(solution)/shard_map/ppermute | solution.py:239
  9.6 1.6 %copy-start = (bf16[1,2,256,2048]{3,2,1,0:T(8,128)(2,1)S(1)}, bf16[1,2,256,2048]{3,2,1,0:T(8,128)(2,1)}, u32[]{:S(2)}) copy-start(bf16[1,2,256,2048]{3,2,1,0:T(8,128)(2,1)} %q_ref.9) | copy-start | bytes 6291460
  13.7 13.5 %collective-permute-start.3 = (bf16[256,1024]{1,0:T(8,128)(2,1)S(1)}, bf16[256,1024]{1,0:T(8,128)(2,1)S(1)}, u32[]{:S(2)}, u32[]{:S(2)}) collective-permute-start(bf16[256,1024]{1,0:T(8,128)(2,1)S(1)} %get-tuple-element.12.x_ref), channel_id=1, source_target_pairs={{0,2},{2,4},{4,6},{6,8},{8,10},{10,12},{12,14},{14,16},{16,18},{18... | collective-permute-start | bytes 1572872 | tf_op jit(solution)/shard_map/ppermute | solution.py:242
  18.4 4.1 %collective-permute-start.2 = (bf16[256,1024]{1,0:T(8,128)(2,1)S(1)}, bf16[256,1024]{1,0:T(8,128)(2,1)S(1)}, u32[]{:S(2)}, u32[]{:S(2)}) collective-permute-start(bf16[256,1024]{1,0:T(8,128)(2,1)S(1)} %collective-permute-done.1.b_ref), channel_id=1, source_target_pairs={{0,1},{1,0},{2,3},{3,2},{4,5},{5,4},{6,7},{7,6},{8,9},{9,8},{10,11... | collective-permute-start | bytes 1572872 | tf_op jit(solution)/shard_map/ppermute | solution.py:245

commit v3 on v2

--- a/solution.py
+++ b/solution.py
@@ -175,14 +175,11 @@
         for half in range(2):
             column = LANES * (2 * group + half)
             x_out[:, column : column + LANES] = out[BLOCK * half : BLOCK * (half + 1)]
-        if group % 2 == 1:
-            columns = pl.ds(4 * LANES * (group // 2), 4 * LANES)
-            copies.append(
-                pltpu.make_async_copy(
-                    x_out.at[:, columns], out_ref.at[0, slot, :, columns], x_sems.at[group // 2]
-                )
-            )
-            copies[-1].start()
+        columns = pl.ds(2 * LANES * group, 2 * LANES)
+        copies.append(
+            pltpu.make_async_copy(x_out.at[:, columns], out_ref.at[0, slot, :, columns], x_sems.at[group])
+        )
+        copies[-1].start()
     for copy in copies:
         copy.wait()
     y_copy.wait()
@@ -240,6 +237,7 @@
     (acc_x,) = call(start_x, 2, [ACC], 1)(queries, x)
     x_late, acc_x = lax.optimization_barrier((x, acc_x))
     a = lax.ppermute(x_late, "seq", forth)
+    queries, acc_x, y = lax.optimization_barrier((queries, acc_x, y))
     (acc_y,) = call(start_y, 3, [ACC], 2)(queries, y, s)
     b, acc_y = lax.optimization_barrier((b, acc_y))
     c = lax.ppermute(b, "seq", swap)
@@ -254,7 +252,7 @@
         scratch_shapes=[
             pltpu.VMEM((BLOCK, WIDTH), BF16),
             pltpu.VMEM((BLOCK, WIDTH), BF16),
-            pltpu.SemaphoreType.DMA((KV_HEADS // 2,)),
+            pltpu.SemaphoreType.DMA((KV_HEADS,)),
             pltpu.SemaphoreType.DMA,
         ],
     )(queries, x, y, s, b, c, a, acc_x, y_done, y_off)

time: 73.5 us -> 73.6 us (level)
  waiting for transfers between devices: 2.19 us -> 3.28 us
  starting transfers between devices: 9.88 us -> 8.87 us
    ppermute x1, starting transfers between devices: 1.48 us -> 0.39 us  [on_device(): c = lax.ppermute(b, 'seq', swap)]
    ppermute x1, waiting for transfers between devices: 2.18 us -> 3.27 us  [on_device(): a = lax.ppermute(x_late, 'seq', forth)]
where the time goes in v3:
time: 73.6 us; the launch traced here: 73.5 us
  Pallas kernels  58.2 us (79%)
  starting transfers between devices  8.87 us (12%)
  waiting for transfers between devices  3.28 us (4%)
  local copies, waits for them, and re-layouts  1.59 us (2%)
  other arithmetic  1.29 us (2%)
    pallas_call x1, Pallas kernels, on_device(): call(finish_x, 10, jax.ShapeDtypeStruct(queries.shape, BF16), 1, out_spec...  46.1 us
    ppermute x1, starting transfers between devices, on_device(): b = lax.ppermute(y, 'seq', back)  8.31 us
    pallas_call x1, Pallas kernels, on_device(): acc_y, = call(start_y, 3, [ACC], 2)(queries, y, s)  4.64 us
    ppermute x1, waiting for transfers between devices, on_device(): a = lax.ppermute(x_late, 'seq', forth)  3.27 us
    pallas_call x1, Pallas kernels, on_device(): y_done, y_off = call(finish_y, 3, [ROWS, OFF], 1)(queries, b, acc_y)  2.57 us
    pallas_call x1, Pallas kernels, on_device(): acc_x, = call(add_near_x, 3, [ACC], 1)(queries, c, acc_x)  2.47 us
    pallas_call x1, Pallas kernels, on_device(): acc_x, = call(start_x, 2, [ACC], 1)(queries, x)  2.45 us
    unnamed x2, local copies, waits for them, and re-layouts  1.59 us
  transfers between devices with their start and end apart: 4, of which 1 were waited for; matrix products, arithmetic and copies ran while one was open for 0% of the time, Pallas kernels for 17%

profile of v3, /device:TPU:24, one launch (start us, length us, event | category | flops | bytes accessed | tf_op | source)
XLA Modules:
  0.0 73.5 jit_solution(6082733981018482746)
XLA Ops:
  0.0 1.3 %fusion.1 = (bf16[256,1024]{1,0:T(8,128)(2,1)S(1)}, bf16[256,1024]{1,0:T(8,128)(2,1)S(1)}) fusion(s32[]{:T(128)S(6)} %select_n.16, bf16[2,256,512]{2,1,0:T(8,128)(2,1)} %bitcast.6, bf16[2,256,512]{2,1,0:T(8,128)(2,1)} %bitcast.7, s32[]{:T(128)S(6)} %select_n.15), kind=kLoop, calls=%fused_computation.5 | loop fusion | flops 2097152 | bytes 2097160 | tf_op jit(solution)/shard_map/jit(dynamic_index_in_dim)/squeeze | solution.py:228
  1.3 0.1 collective-permute-start
  1.4 8.3 %collective-permute-start.1 = (bf16[256,1024]{1,0:T(8,128)(2,1)S(1)}, bf16[256,1024]{1,0:T(8,128)(2,1)S(1)}, u32[]{:S(2)}, u32[]{:S(2)}) collective-permute-start(bf16[256,1024]{1,0:T(8,128)(2,1)S(1)} %get-tuple-element.16.y_ref), channel_id=1, source_target_pairs={{1,3},{3,5},{5,7},{7,9},{9,11},{11,13},{13,15},{15,17},{17,19},{19... | collective-permute-start | bytes 1572872 | tf_op jit(solution)/shard_map/ppermute | solution.py:235
  9.7 0.0 copy-start
  9.7 1.6 %copy-done = bf16[1,2,256,2048]{3,2,1,0:T(8,128)(2,1)S(1)} copy-done((bf16[1,2,256,2048]{3,2,1,0:T(8,128)(2,1)S(1)}, bf16[1,2,256,2048]{3,2,1,0:T(8,128)(2,1)}, u32[]{:S(2)}) %copy-start) | copy-done | bytes 2097176
  11.3 2.4 %shard_map.37.acc_in = f32[8,2,512,128]{3,2,1,0:T(8,128)S(1)} custom-call(bf16[1,2,256,2048]{3,2,1,0:T(8,128)(2,1)S(1)} %copy-done, bf16[256,1024]{1,0:T(8,128)(2,1)S(1)} %get-tuple-element.18.x_ref), custom_call_target="tpu_custom_call" | custom-call | flops 10000000000 | bytes 1024 | tf_op jit(solution)/shard_map/pallas_call | solution.py:237
  13.8 0.1 collective-permute-start.3
  13.9 0.0 collective-permute-done.s_ref
  13.9 4.6 %shard_map.38.acc_in = f32[8,2,512,128]{3,2,1,0:T(8,128)S(1)} custom-call(bf16[1,2,256,2048]{3,2,1,0:T(8,128)(2,1)S(1)} %copy-done, bf16[256,1024]{1,0:T(8,128)(2,1)S(1)} %get-tuple-element.16.y_ref, bf16[256,1024]{1,0:T(8,128)(2,1)S(1)} %collective-permute-done.s_ref), custom_call_target="tpu_custom_call" | custom-call | flops 20000000000 | bytes 1024 | tf_op jit(solution)/shard_map/pallas_call | solution.py:241
  18.5 0.0 collective-permute-done.1.b_ref
  18.5 0.4 collective-permute-start.2
  18.9 2.6 %shard_map.40 = (bf16[256,2048]{1,0:T(8,128)(2,1)S(1)}, f32[8,128]{1,0:T(8,128)S(1)}) custom-call(bf16[1,2,256,2048]{3,2,1,0:T(8,128)(2,1)S(1)} %copy-done, bf16[256,1024]{1,0:T(8,128)(2,1)S(1)} %collective-permute-done.1.b_ref, f32[8,2,512,128]{3,2,1,0:T(8,128)S(1)} %shard_map.38.acc_in), custom_call_target="tpu_custom_call" | custom-call | flops 10000000000 | bytes 1024 | tf_op jit(solution)/shard_map/pallas_call | solution.py:244
  21.5 0.0 collective-permute-done.2.c_ref
  21.5 2.5 %shard_map.39.acc_in = f32[8,2,512,128]{3,2,1,0:T(8,128)S(1)} custom-call(bf16[1,2,256,2048]{3,2,1,0:T(8,128)(2,1)S(1)} %copy-done, bf16[256,1024]{1,0:T(8,128)(2,1)S(1)} %collective-permute-done.2.c_ref, f32[8,2,512,128]{3,2,1,0:T(8,128)S(1)} %shard_map.37.acc_in), custom_call_target="tpu_custom_call" | custom-call | flops 10000000000 | bytes 1024 | tf_op jit(solution)/shard_map/pallas_call | solution.py:245
  24.0 3.3 %collective-permute-done.3.a_ref = bf16[256,1024]{1,0:T(8,128)(2,1)S(1)} collective-permute-done((bf16[256,1024]{1,0:T(8,128)(2,1)S(1)}, bf16[256,1024]{1,0:T(8,128)(2,1)S(1)}, u32[]{:S(2)}, u32[]{:S(2)}) %collective-permute-start.3) | collective-permute-done | bytes 524320 | tf_op jit(solution)/shard_map/ppermute | solution.py:239
  27.2 46.1 %shard_map.41 = bf16[1,2,256,2048]{3,2,1,0:T(8,128)(2,1)} custom-call(bf16[1,2,256,2048]{3,2,1,0:T(8,128)(2,1)S(1)} %copy-done, bf16[256,1024]{1,0:T(8,128)(2,1)S(1)} %get-tuple-element.18.x_ref, bf16[256,1024]{1,0:T(8,128)(2,1)S(1)} %get-tuple-element.16.y_ref, bf16[256,1024]{1,0:T(8,128)(2,1)S(1)} %collective-permute-done.s_ref, ...), custom_call_target="tpu_custom_call" | custom-call | flops 10000000000 | bytes 1024 | tf_op jit(solution)/shard_map/pallas_call | solution.py:246
Async XLA Ops:
  1.3 12.6 %collective-permute-start = (bf16[256,1024]{1,0:T(8,128)(2,1)S(1)}, bf16[256,1024]{1,0:T(8,128)(2,1)S(1)}, u32[]{:S(2)}, u32[]{:S(2)}) collective-permute-start(bf16[256,1024]{1,0:T(8,128)(2,1)S(1)} %get-tuple-element.18.x_ref), channel_id=1, source_target_pairs={{0,1},{1,0},{2,3},{3,2},{4,5},{5,4},{6,7},{7,6},{8,9},{9,8},{10,11... | collective-permute-start | bytes 1572872 | tf_op jit(solution)/shard_map/ppermute | solution.py:236
  1.4 17.1 %collective-permute-start.1 = (bf16[256,1024]{1,0:T(8,128)(2,1)S(1)}, bf16[256,1024]{1,0:T(8,128)(2,1)S(1)}, u32[]{:S(2)}, u32[]{:S(2)}) collective-permute-start(bf16[256,1024]{1,0:T(8,128)(2,1)S(1)} %get-tuple-element.16.y_ref), channel_id=1, source_target_pairs={{1,3},{3,5},{5,7},{7,9},{9,11},{11,13},{13,15},{15,17},{17,19},{19... | collective-permute-start | bytes 1572872 | tf_op jit(solution)/shard_map/ppermute | solution.py:235
  9.7 1.6 %copy-start = (bf16[1,2,256,2048]{3,2,1,0:T(8,128)(2,1)S(1)}, bf16[1,2,256,2048]{3,2,1,0:T(8,128)(2,1)}, u32[]{:S(2)}) copy-start(bf16[1,2,256,2048]{3,2,1,0:T(8,128)(2,1)} %q_ref.5) | copy-start | bytes 6291460
  13.8 13.5 %collective-permute-start.3 = (bf16[256,1024]{1,0:T(8,128)(2,1)S(1)}, bf16[256,1024]{1,0:T(8,128)(2,1)S(1)}, u32[]{:S(2)}, u32[]{:S(2)}) collective-permute-start(bf16[256,1024]{1,0:T(8,128)(2,1)S(1)} %get-tuple-element.18.x_ref), channel_id=1, source_target_pairs={{0,2},{2,4},{4,6},{6,8},{8,10},{10,12},{12,14},{14,16},{16,18},{18... | collective-permute-start | bytes 1572872 | tf_op jit(solution)/shard_map/ppermute | solution.py:239
  18.5 3.0 %collective-permute-start.2 = (bf16[256,1024]{1,0:T(8,128)(2,1)S(1)}, bf16[256,1024]{1,0:T(8,128)(2,1)S(1)}, u32[]{:S(2)}, u32[]{:S(2)}) collective-permute-start(bf16[256,1024]{1,0:T(8,128)(2,1)S(1)} %collective-permute-done.1.b_ref), channel_id=1, source_target_pairs={{0,1},{1,0},{2,3},{3,2},{4,5},{5,4},{6,7},{7,6},{8,9},{9,8},{10,11... | collective-permute-start | bytes 1572872 | tf_op jit(solution)/shard_map/ppermute | solution.py:243

commit v4 on v2

--- a/solution.py
+++ b/solution.py
@@ -22,6 +22,7 @@
 TOTAL_LOW = 2.0**-80
 TOTAL_HIGH = 2.0**100
 MIB = 2**20
+RUN = 16
 FLOPS = 10**10
 
 
@@ -80,6 +81,16 @@
     return out, jnp.max(off, axis=0, keepdims=True)
 
 
+def in_early_chip():
+    index = lax.axis_index("seq")
+    return (index % RUN < 2) & (index >= RUN)
+
+
+def early_and_odd():
+    index = lax.axis_index("seq")
+    return (index % RUN == 1) & (index >= RUN)
+
+
 def start_x(q_ref, x_ref, acc):
     slot = lax.axis_index("seq") % 2
     for group in range(KV_HEADS):
@@ -87,11 +98,41 @@
         acc[group, 0], acc[group, 1] = sums
 
 
-def start_y(q_ref, y_ref, s_ref, acc):
+def start_y(q_ref, kv_refs, acc):
     slot = 1 - lax.axis_index("seq") % 2
     for group in range(KV_HEADS):
-        sums = partial_sums(group_queries(q_ref, slot, group), [y_ref, s_ref], group, diagonal=True)
+        sums = partial_sums(group_queries(q_ref, slot, group), kv_refs, group, diagonal=True)
         acc[group, 0], acc[group, 1] = sums
+
+
+def start_early(q_ref, x_ref, acc_x):
+    @pl.when(in_early_chip())
+    def _():
+        start_x(q_ref, x_ref, acc_x)
+
+
+def start_late(q_ref, x_ref, y_ref, acc_x_in, acc_x, acc_y):
+    @pl.when(~in_early_chip())
+    def _():
+        start_x(q_ref, x_ref, acc_x)
+
+    @pl.when(early_and_odd())
+    def _():
+        start_y(q_ref, [y_ref], acc_y)
+
+
+def near_y(q_ref, y_ref, s_ref, acc_in, acc):
+    @pl.when(~early_and_odd())
+    def _():
+        start_y(q_ref, [y_ref, s_ref], acc)
+
+    @pl.when(early_and_odd())
+    def _():
+        slot = 1 - lax.axis_index("seq") % 2
+        for group in range(KV_HEADS):
+            sums = partial_sums(group_queries(q_ref, slot, group), [s_ref], group)
+            for parity in range(2):
+                acc[group, parity] = acc_in[group, parity] + sums[parity]
 
 
 def valid_from(first):
@@ -235,12 +276,14 @@
     ring = odds + evens[::-1]
     back = list(zip(ring, ring[1:] + ring[:1]))
     swap = [(i, i ^ 1) for i in range(count)]
-    b = lax.ppermute(y, "seq", back)
     s = lax.ppermute(x, "seq", swap)
-    (acc_x,) = call(start_x, 2, [ACC], 1)(queries, x)
+    (acc_x,) = call(start_early, 2, [ACC], 1)(queries, x)
+    y_late, acc_x = lax.optimization_barrier((y, acc_x))
+    b = lax.ppermute(y_late, "seq", back)
+    acc_x, acc_y = call(start_late, 4, [ACC, ACC], 1, input_output_aliases={3: 0})(queries, x, y, acc_x)
     x_late, acc_x = lax.optimization_barrier((x, acc_x))
     a = lax.ppermute(x_late, "seq", forth)
-    (acc_y,) = call(start_y, 3, [ACC], 2)(queries, y, s)
+    (acc_y,) = call(near_y, 4, [ACC], 2, input_output_aliases={3: 0})(queries, y, s, acc_y)
     b, acc_y = lax.optimization_barrier((b, acc_y))
     c = lax.ppermute(b, "seq", swap)
     y_done, y_off = call(finish_y, 3, [ROWS, OFF], 1)(queries, b, acc_y)

time: 73.5 us -> 73.3 us (level)
  starting transfers between devices: 9.88 us -> 5.87 us
  waiting for transfers between devices: 2.19 us -> 5.27 us
    ppermute x1, waiting for transfers between devices: 0.01 us -> 5.26 us  [on_device(): b = lax.ppermute(y_late, 'seq', back)]
    ppermute x1, starting transfers between devices: 8.31 us -> 5.77 us  [on_device(): b = lax.ppermute(y_late, 'seq', back)]
    ppermute x1, waiting for transfers between devices: 2.18 us -> 0.01 us  [on_device(): a = lax.ppermute(x_late, 'seq', forth)]
    ppermute x1, starting transfers between devices: 1.48 us -> 0.01 us  [on_device(): c = lax.ppermute(b, 'seq', swap)]
    pallas_call x2 -> x3, Pallas kernels: 7.09 us -> 7.09 us  [the longest x1 4.64 us: on_device(): call(near_y, 4, [ACC], 2, input_output_aliases={3: 0})(queries, y, s, acc_y)]
where the time goes in v4:
time: 73.3 us; the launch traced here: 72.5 us
  Pallas kernels  58.2 us (79%)
  starting transfers between devices  5.87 us (8%)
  waiting for transfers between devices  5.27 us (7%)
  local copies, waits for them, and re-layouts  1.59 us (2%)
  other arithmetic  1.29 us (2%)
    pallas_call x1, Pallas kernels, on_device(): call(finish_x, 10, jax.ShapeDtypeStruct(queries.shape, BF16), 1, out_spec...  46.1 us
    ppermute x1, starting transfers between devices, on_device(): b = lax.ppermute(y_late, 'seq', back)  5.77 us
    ppermute x1, waiting for transfers between devices, on_device(): b = lax.ppermute(y_late, 'seq', back)  5.26 us
    pallas_call x1, Pallas kernels, on_device(): call(near_y, 4, [ACC], 2, input_output_aliases={3: 0})(queries, y, s, acc_y)  4.64 us
    pallas_call x1, Pallas kernels, on_device(): y_done, y_off = call(finish_y, 3, [ROWS, OFF], 1)(queries, b, acc_y)  2.57 us
    pallas_call x1, Pallas kernels, on_device(): acc_x, = call(add_near_x, 3, [ACC], 1)(queries, c, acc_x)  2.47 us
    pallas_call x1, Pallas kernels, on_device(): acc_x, = call(start_early, 2, [ACC], 1)(queries, x)  2.45 us
    unnamed x2, local copies, waits for them, and re-layouts  1.59 us
  transfers between devices with their start and end apart: 4, of which 1 were waited for; matrix products, arithmetic and copies ran while one was open for 0% of the time, Pallas kernels for 17%

profile of v4, /device:TPU:24, one launch (start us, length us, event | category | flops | bytes accessed | tf_op | source)
XLA Modules:
  0.0 72.5 jit_solution(11364832998733955388)
XLA Ops:
  0.0 1.3 %fusion.1 = (bf16[256,1024]{1,0:T(8,128)(2,1)S(1)}, bf16[256,1024]{1,0:T(8,128)(2,1)S(1)}) fusion(s32[]{:T(128)S(6)} %select_n.16, bf16[2,256,512]{2,1,0:T(8,128)(2,1)} %bitcast.6, bf16[2,256,512]{2,1,0:T(8,128)(2,1)} %bitcast.7, s32[]{:T(128)S(6)} %select_n.15), kind=kLoop, calls=%fused_computation.5 | loop fusion | flops 2097152 | bytes 2097160 | tf_op jit(solution)/shard_map/jit(dynamic_index_in_dim)/squeeze | solution.py:272
  1.3 0.1 collective-permute-start
  1.4 0.0 copy-start
  1.4 1.6 %copy-done = bf16[1,2,256,2048]{3,2,1,0:T(8,128)(2,1)S(1)} copy-done((bf16[1,2,256,2048]{3,2,1,0:T(8,128)(2,1)S(1)}, bf16[1,2,256,2048]{3,2,1,0:T(8,128)(2,1)}, u32[]{:S(2)}) %copy-start) | copy-done | bytes 2097176
  3.0 2.5 %shard_map.37.acc_x_in = f32[8,2,512,128]{3,2,1,0:T(8,128)S(1)} custom-call(bf16[1,2,256,2048]{3,2,1,0:T(8,128)(2,1)S(1)} %copy-done, bf16[256,1024]{1,0:T(8,128)(2,1)S(1)} %get-tuple-element.20.x_ref), custom_call_target="tpu_custom_call" | custom-call | flops 10000000000 | bytes 1024 | tf_op jit(solution)/shard_map/pallas_call | solution.py:280
  5.5 5.8 %collective-permute-start.1 = (bf16[256,1024]{1,0:T(8,128)(2,1)S(1)}, bf16[256,1024]{1,0:T(8,128)(2,1)S(1)}, u32[]{:S(2)}, u32[]{:S(2)}) collective-permute-start(bf16[256,1024]{1,0:T(8,128)(2,1)S(1)} %get-tuple-element.15.y_ref), channel_id=1, source_target_pairs={{1,3},{3,5},{5,7},{7,9},{9,11},{11,13},{13,15},{15,17},{17,19},{19... | collective-permute-start | bytes 1572872 | tf_op jit(solution)/shard_map/ppermute | solution.py:282
  11.2 0.0 collective-permute-start.3
  11.2 0.0 collective-permute-done.s_ref
  11.2 4.6 %shard_map.39.acc_in = f32[8,2,512,128]{3,2,1,0:T(8,128)S(1)} custom-call(bf16[1,2,256,2048]{3,2,1,0:T(8,128)(2,1)S(1)} %copy-done, bf16[256,1024]{1,0:T(8,128)(2,1)S(1)} %get-tuple-element.15.y_ref, bf16[256,1024]{1,0:T(8,128)(2,1)S(1)} %collective-permute-done.s_ref, f32[8,2,512,128]{3,2,1,0:T(8,128)S(1)} %get-tuple-element.17.acc_in), custom_call_target="tpu_custom_call", output_to_operand_aliasing={{}: (3, {})} | custom-call | flops 20000000000 | bytes 1024 | tf_op jit(solution)/shard_map/pallas_call | solution.py:286
  15.9 5.3 %collective-permute-done.1.b_ref = bf16[256,1024]{1,0:T(8,128)(2,1)S(1)} collective-permute-done((bf16[256,1024]{1,0:T(8,128)(2,1)S(1)}, bf16[256,1024]{1,0:T(8,128)(2,1)S(1)}, u32[]{:S(2)}, u32[]{:S(2)}) %collective-permute-start.1) | collective-permute-done | bytes 524320 | tf_op jit(solution)/shard_map/ppermute | solution.py:282
  21.1 0.0 collective-permute-start.2
  21.1 2.6 %shard_map.41 = (bf16[256,2048]{1,0:T(8,128)(2,1)S(1)}, f32[8,128]{1,0:T(8,128)S(1)}) custom-call(bf16[1,2,256,2048]{3,2,1,0:T(8,128)(2,1)S(1)} %copy-done, bf16[256,1024]{1,0:T(8,128)(2,1)S(1)} %collective-permute-done.1.b_ref, f32[8,2,512,128]{3,2,1,0:T(8,128)S(1)} %shard_map.39.acc_in), custom_call_target="tpu_custom_call" | custom-call | flops 10000000000 | bytes 1024 | tf_op jit(solution)/shard_map/pallas_call | solution.py:289
  23.7 0.0 collective-permute-done.2.c_ref
  23.7 2.5 %shard_map.40.acc_in = f32[8,2,512,128]{3,2,1,0:T(8,128)S(1)} custom-call(bf16[1,2,256,2048]{3,2,1,0:T(8,128)(2,1)S(1)} %copy-done, bf16[256,1024]{1,0:T(8,128)(2,1)S(1)} %collective-permute-done.2.c_ref, f32[8,2,512,128]{3,2,1,0:T(8,128)S(1)} %get-tuple-element.21.acc_in), custom_call_target="tpu_custom_call" | custom-call | flops 10000000000 | bytes 1024 | tf_op jit(solution)/shard_map/pallas_call | solution.py:290
  26.2 0.0 collective-permute-done.3.a_ref
  26.2 46.1 %shard_map.42 = bf16[1,2,256,2048]{3,2,1,0:T(8,128)(2,1)} custom-call(bf16[1,2,256,2048]{3,2,1,0:T(8,128)(2,1)S(1)} %copy-done, bf16[256,1024]{1,0:T(8,128)(2,1)S(1)} %get-tuple-element.20.x_ref, bf16[256,1024]{1,0:T(8,128)(2,1)S(1)} %get-tuple-element.15.y_ref, bf16[256,1024]{1,0:T(8,128)(2,1)S(1)} %collective-permute-done.s_ref, ...), custom_call_target="tpu_custom_call" | custom-call | flops 10000000000 | bytes 1024 | tf_op jit(solution)/shard_map/pallas_call | solution.py:291
  (1 shorter events, 0.0 us)
Async XLA Ops:
  1.3 9.9 %collective-permute-start = (bf16[256,1024]{1,0:T(8,128)(2,1)S(1)}, bf16[256,1024]{1,0:T(8,128)(2,1)S(1)}, u32[]{:S(2)}, u32[]{:S(2)}) collective-permute-start(bf16[256,1024]{1,0:T(8,128)(2,1)S(1)} %get-tuple-element.20.x_ref), channel_id=1, source_target_pairs={{0,1},{1,0},{2,3},{3,2},{4,5},{5,4},{6,7},{7,6},{8,9},{9,8},{10,11... | collective-permute-start | bytes 1572872 | tf_op jit(solution)/shard_map/ppermute | solution.py:279
  1.4 1.6 %copy-start = (bf16[1,2,256,2048]{3,2,1,0:T(8,128)(2,1)S(1)}, bf16[1,2,256,2048]{3,2,1,0:T(8,128)(2,1)}, u32[]{:S(2)}) copy-start(bf16[1,2,256,2048]{3,2,1,0:T(8,128)(2,1)} %q_ref.11) | copy-start | bytes 6291460
  5.5 15.7 %collective-permute-start.1 = (bf16[256,1024]{1,0:T(8,128)(2,1)S(1)}, bf16[256,1024]{1,0:T(8,128)(2,1)S(1)}, u32[]{:S(2)}, u32[]{:S(2)}) collective-permute-start(bf16[256,1024]{1,0:T(8,128)(2,1)S(1)} %get-tuple-element.15.y_ref), channel_id=1, source_target_pairs={{1,3},{3,5},{5,7},{7,9},{9,11},{11,13},{13,15},{15,17},{17,19},{19... | collective-permute-start | bytes 1572872 | tf_op jit(solution)/shard_map/ppermute | solution.py:282
  11.2 15.0 %collective-permute-start.3 = (bf16[256,1024]{1,0:T(8,128)(2,1)S(1)}, bf16[256,1024]{1,0:T(8,128)(2,1)S(1)}, u32[]{:S(2)}, u32[]{:S(2)}) collective-permute-start(bf16[256,1024]{1,0:T(8,128)(2,1)S(1)} %get-tuple-element.20.x_ref), channel_id=1, source_target_pairs={{0,2},{2,4},{4,6},{6,8},{8,10},{10,12},{12,14},{14,16},{16,18},{18... | collective-permute-start | bytes 1572872 | tf_op jit(solution)/shard_map/ppermute | solution.py:285
  21.1 2.6 %collective-permute-start.2 = (bf16[256,1024]{1,0:T(8,128)(2,1)S(1)}, bf16[256,1024]{1,0:T(8,128)(2,1)S(1)}, u32[]{:S(2)}, u32[]{:S(2)}) collective-permute-start(bf16[256,1024]{1,0:T(8,128)(2,1)S(1)} %collective-permute-done.1.b_ref), channel_id=1, source_target_pairs={{0,1},{1,0},{2,3},{3,2},{4,5},{5,4},{6,7},{7,6},{8,9},{9,8},{10,11... | collective-permute-start | bytes 1572872 | tf_op jit(solution)/shard_map/ppermute | solution.py:288
